TPU v7x, 32 devices: a whole 2x2x4 slice. The times are simulated.
32 devices in a mesh: dp: 2 (over x), ctx: 4 (over y, core), exp: 4 (over z).
Axes of the slice: x: 2, y: 2, z: 4, core: 2. Of those that a mesh axis runs over, the one named last changes fastest.
Arguments:
- queries: bfloat16 [2, 1024, 3584], P('dp', 'ctx'), may hold values from -20 to 20
- keys: bfloat16 [2, 1024, 512], P('dp', 'ctx'), may hold values from -20 to 20
- values: bfloat16 [2, 1024, 512], P('dp', 'ctx'), may hold values from -6 to 6
- residual: bfloat16 [2, 1024, 3584], P('dp', 'ctx'), may hold values from -4 to 4
- labels: int32 [2, 8], P('dp'), may hold values from 0 to 1, as said below
- block_mask: int32 [2, 8, 8], P('dp'), may hold values from 0 to 1, as said below
- gains: float32 [2, 3584], replicated, may hold values from 0.5 to 1.5
- w_gate: bfloat16 [3584, 1216], P(None, 'exp'), may hold values from -0.09375 to 0.09375
- w_up: bfloat16 [3584, 1216], P(None, 'exp'), may hold values from -0.09375 to 0.09375
- w_down: bfloat16 [1216, 3584], P('exp'), may hold values from -0.625 to 0.625
Outputs:
- layer_out: bfloat16 [2, 1024, 3584], P('dp', ('ctx', 'exp'))
Inputs may be any that keep to these rules, and one draw needn't show every extreme that they name: `labels`: per sequence a share of visual blocks is drawn, then each block's label independently. Each sequence is packed with documents made of whole blocks, the first starting at block 0. block_mask[i, j] is 1 exactly when blocks i and j lie in the same document and (j <= i, or blocks i and j are both visual with no text block between them); the diagonal is always 1.
All inputs are finite; a program needn't handle non-finite values.
Results may differ from a plain program's by a relative error of at most 0.0069.
Values may be sent and summed in bfloat16 or wider, within the bound.
No kernel may reach another device: no remote copies, remote signals or barrier semaphores. Data moves between devices by JAX's collectives and lax.ppermute only.
A program may use at most 64 MiB of HBM per device.

v0:
```python
import jax
import jax.numpy as jnp
from jax import lax
from jax.sharding import PartitionSpec as P

KV_HEADS = 4
HEAD_DIM = 128
BLOCK = 128


def per_device(queries, keys, values, residual, labels, block_mask, gains, w_gate, w_up, w_down):
    shard = queries.shape[1]
    width = queries.shape[2]
    group = width // (KV_HEADS * HEAD_DIM)
    head_width = group * HEAD_DIM
    exp_count = lax.axis_size("exp")
    exp_here = lax.axis_index("exp")
    slices = exp_count // KV_HEADS
    rows_sub = shard // slices
    slice_id = exp_here // KV_HEADS
    head_id = exp_here % KV_HEADS
    shard_base = lax.axis_index("ctx") * shard
    labels_row = labels[0]
    block_count = labels_row.shape[0]
    block_ids = jnp.arange(block_count, dtype=jnp.int32)
    labels_float = labels_row.astype(jnp.float32)
    mask_float = block_mask[0].astype(jnp.float32)
    q_first = slice_id * rows_sub
    q_local = lax.dynamic_slice(
        queries[0], (q_first, head_id * head_width), (rows_sub, head_width)
    ).reshape(rows_sub, group, HEAD_DIM)
    q_pos = shard_base + q_first + jnp.arange(rows_sub, dtype=jnp.int32)
    q_blk = q_pos // BLOCK
    q_onehot = (q_blk[:, None] == block_ids[None, :]).astype(jnp.float32)
    q_mask_rows = jnp.dot(q_onehot, mask_float)
    q_visual = jnp.dot(q_onehot, labels_float)
    scale = 1.0 / jnp.sqrt(jnp.float32(HEAD_DIM))
    whole_keys, whole_values = (
        lax.all_gather(keys, "ctx", axis=1, tiled=True),
        lax.all_gather(values, "ctx", axis=1, tiled=True),
    )
    count = whole_keys.shape[1]
    k_head = lax.dynamic_slice_in_dim(whole_keys[0], head_id * HEAD_DIM, HEAD_DIM, 1)
    v_head = lax.dynamic_slice_in_dim(whole_values[0], head_id * HEAD_DIM, HEAD_DIM, 1)
    k_pos = jnp.arange(count, dtype=jnp.int32)
    k_blk = k_pos // BLOCK
    k_onehot = (block_ids[:, None] == k_blk[None, :]).astype(jnp.float32)
    block_ok = jnp.dot(q_mask_rows, k_onehot) > 0.5
    allowed = block_ok & (
        (k_blk[None, :] != q_blk[:, None])
        | (k_pos[None, :] <= q_pos[:, None])
        | (q_visual[:, None] > 0.5)
    )
    scores = jnp.einsum("qrd,kd->rqk", q_local, k_head, preferred_element_type=jnp.float32) * scale
    scores = jnp.where(allowed[None], scores, -1e30)
    run_max = jnp.full((group, rows_sub), -1e30, jnp.float32)
    new_max = jnp.maximum(run_max, jnp.max(scores, axis=-1))
    weights = jnp.where(allowed[None], jnp.exp(scores - new_max[..., None]), 0.0)
    total = jnp.sum(weights, axis=-1)
    soft = weights.astype(jnp.bfloat16)
    accum = jnp.einsum("rqk,kd->rqd", soft, v_head, preferred_element_type=jnp.float32)
    attended = accum / total[..., None]
    own_part = jnp.transpose(attended, (1, 0, 2)).reshape(rows_sub, head_width).astype(jnp.bfloat16)
    collected = lax.all_gather(own_part[None], "exp", axis=0, tiled=True)
    attention = jnp.transpose(
        collected.reshape(slices, KV_HEADS, rows_sub, head_width), (0, 2, 1, 3)
    ).reshape(shard, width)
    mid = residual[0].astype(jnp.float32) + attention.astype(jnp.float32)
    row_blk = (shard_base + jnp.arange(shard, dtype=jnp.int32)) // BLOCK
    row_visual = jnp.dot((row_blk[:, None] == block_ids[None, :]).astype(jnp.float32), labels_float)
    gain_rows = jnp.where(row_visual[:, None] > 0.5, gains[1][None, :], gains[0][None, :])
    normed = (
        mid * lax.rsqrt(jnp.mean(mid * mid, axis=-1, keepdims=True) + 1e-05) * gain_rows
    ).astype(jnp.bfloat16)
    section = (exp_here >= exp_count // 2).astype(jnp.float32)
    keep = (row_visual == section).astype(jnp.float32)
    gate = jnp.dot(normed, w_gate, preferred_element_type=jnp.float32)
    upper = jnp.dot(normed, w_up, preferred_element_type=jnp.float32)
    hidden = (jax.nn.silu(gate) * upper).astype(jnp.bfloat16)
    partial_terms = jnp.dot(hidden, w_down, preferred_element_type=jnp.float32) * keep[:, None]
    branch = lax.psum_scatter(partial_terms[None], "exp", scatter_dimension=1, tiled=True)
    out_rows = shard // exp_count
    mid_rows = lax.dynamic_slice_in_dim(mid, exp_here * out_rows, out_rows, 0)
    return (mid_rows[None] + branch).astype(jnp.bfloat16)


def solution(mesh):
    placed = (
        P("dp", "ctx", None),
        P("dp", "ctx", None),
        P("dp", "ctx", None),
        P("dp", "ctx", None),
        P("dp", None),
        P("dp", None, None),
        P(),
        P(None, "exp"),
        P(None, "exp"),
        P("exp", None),
    )
    return jax.shard_map(
        per_device,
        mesh=mesh,
        in_specs=placed,
        out_specs=P("dp", ("ctx", "exp"), None),
        check_vma=False,
    )
```

profile of v0, /device:TPU:14, one launch (start us, length us, event | category | flops | bytes accessed | tf_op | source)
XLA Modules:
  0.0 186.6 jit_solution(15146607740484781796)
XLA Ops:
  6.5 0.0 copy-start
  6.5 0.0 all-gather.4.cloned.1.call-start
  6.5 0.7 all-gather.4.cloned.1.call-update
  7.3 0.0 all-gather.6.cloned.1.call-start
  7.3 0.7 all-gather.6.cloned.1.call-update
  8.0 0.0 all-gather.8.cloned.1.call-start
  8.1 0.9 fusion.34
  9.0 1.1 constant_dynamic-slice_fusion.1
  10.1 0.2 copy.38
  10.3 1.4 fusion.10
  11.7 0.4 copy.28
  12.2 13.6 %all-gather.4.cloned.1.call-done = bf16[1,1024,512]{2,1,0:T(8,128)(2,1)} async-done(((bf16[1,256,512]{2,1,0:T(8,128)(2,1)}), bf16[1,1024,512]{2,1,0:T(8,128)(2,1)}) %all-gather.4.cloned.1.call-update) | async-done | bytes 1048592 | tf_op jit(solution)/shard_map/all_gather | solution.py:39
  25.9 2.2 %fusion = (f32[7,256]{1,0:T(8,128)S(1)}, f32[1024,256,7]{1,0,2:T(8,128)S(1)}) fusion(pred[256,1024]{0,1:T(8,128)(4,1)S(1)} %copy.28, bf16[256,7,128]{0,2,1:T(8,128)(2,1)S(1)} %bitcast.74, bf16[1,1024,512]{2,1,0:T(8,128)(2,1)} %all-gather.4.cloned.1.call-done, s32[]{:T(128)S(6)} %select_n.64), kind=kOutput, calls=%fused_computation.2 | convolution fusion | flops 475265280 | bytes 8330244 | tf_op jit(solution)/shard_map/qrd,kd->rqk/dot_general | solution.py:54
  28.1 0.0 copy-start.1
  28.1 2.9 %copy-done.1 = f32[1024,256,7]{1,0,2:T(8,128)} copy-done((f32[1024,256,7]{1,0,2:T(8,128)}, f32[1024,256,7]{1,0,2:T(8,128)S(1)}, u32[]{:S(2)}) %copy-start.1) | copy-done | bytes 7340056
  31.0 1.8 fusion.2
  32.8 11.4 %all-gather.6.cloned.1.call-done = bf16[1,1024,512]{2,1,0:T(8,128)(2,1)} async-done(((bf16[1,256,512]{2,1,0:T(8,128)(2,1)}), bf16[1,1024,512]{2,1,0:T(8,128)(2,1)}) %all-gather.6.cloned.1.call-update) | async-done | bytes 1048592 | tf_op jit(solution)/shard_map/all_gather | solution.py:40
  44.2 5.3 %fusion.19 = bf16[256,7,128]{0,2,1:T(8,128)(2,1)S(1)} fusion(f32[1024,256,7]{1,0,2:T(8,128)} %copy-done.1, f32[7,256]{1,0:T(8,128)S(1)} %broadcast_maximum_fusion, pred[256,1024]{0,1:T(8,128)(4,1)S(1)} %copy.28, f32[256,7]{0,1:T(8,128)S(1)} %bitcast.76, bf16[1,1024,512]{2,1,0:T(8,128)(2,1)} %all-gather.6.cloned.1.call-done, s32[]{:T(128)S(6)} %select_n.64), kind=kOutput, calls=%fused_computation.23 | convolution fusion | flops 479395840 | bytes 8337412 | tf_op jit(solution)/shard_map/rqk,kd->rqd/dot_general | solution.py:61
  49.4 0.0 copy-start.5
  49.4 0.0 copy-start.7
  49.5 1.0 copy.33
  50.4 0.0 all-gather.8.cloned.1.call-update
  50.5 0.2 reduce-scatter.2.cloned.1.call-start
  50.7 3.8 %copy.27 = bf16[1,256,3584]{1,2,0:T(8,128)(2,1)} copy(bf16[1,256,3584]{2,1,0:T(8,128)(2,1)} %param.13) | data formatting | bytes 3670016 | tf_op args[3]
  54.5 0.0 copy-done.5
  54.5 0.1 slice_reduce_fusion.1
  54.6 0.0 copy-done.7
  54.6 0.2 fusion.35
  54.8 36.9 %all-gather.8.cloned.1.call-done = bf16[4,256,896]{2,1,0:T(8,128)(2,1)} async-done(((bf16[1,256,896]{2,1,0:T(8,128)(2,1)}), bf16[4,256,896]{2,1,0:T(8,128)(2,1)}) %all-gather.8.cloned.1.call-update) | async-done | bytes 1835024 | tf_op jit(solution)/shard_map/all_gather | solution.py:64
  91.7 3.6 %copy.34 = bf16[4,256,896]{1,2,0:T(8,128)(2,1)} copy(bf16[4,256,896]{2,1,0:T(8,128)(2,1)} %all-gather.8.cloned.1.call-done) | data formatting | bytes 3670016 | tf_op jit(solution)/shard_map/all_gather | solution.py:64
  95.3 0.0 copy-start.3
  95.3 1.9 %bitcast_convert_fusion = f32[1,4,256,896]{2,3,1,0:T(8,128)S(1)} fusion(bf16[4,256,896]{1,2,0:T(8,128)(2,1)} %copy.34), kind=kLoop, calls=%fused_computation.12 | loop fusion | flops 917504 | bytes 5505024 | tf_op jit(solution)/shard_map/convert_element_type | solution.py:68
  97.3 0.1 copy-done.3
  97.4 0.5 multiply_reduce_fusion
  97.9 0.0 copy-start.2
  97.9 0.0 copy-start.6
  97.9 2.7 %multiply_convert_fusion = bf16[256,3584]{0,1:T(8,128)(2,1)S(1)} fusion(f32[256,3584]{0,1:T(8,128)S(1)} %get-tuple-element.8, f32[3584]{0:T(1024)S(1)} %get-tuple-element.6, f32[3584]{0:T(1024)S(1)} %get-tuple-element.5, f32[256]{0:T(256)S(1)} %add_rsqrt_fusion, pred[256]{0:T(512)(128)(4,1)S(1)} %get-tuple-element.9), kind=kLoop, calls=%fused_computation.8 | loop fusion | flops 3670016 | bytes 5534976 | tf_op jit(solution)/shard_map/convert_element_type | solution.py:74
  100.6 0.0 copy-start.4
  100.6 1.3 copy-done.4
  101.9 0.0 copy-done.6
  101.9 0.7 fusion.58
  102.7 0.0 copy-done.2
  102.7 0.0 copy-done
  102.7 6.9 %fusion.1 = f32[1,256,3584]{2,1,0:T(8,128)} fusion(bf16[304,3584]{1,0:T(8,128)(2,1)S(1)} %copy-done, f32[256]{0:T(256)S(1)} %get-tuple-element.10, bf16[3584,304]{0,1:T(8,128)(2,1)} %param.18, bf16[256,3584]{0,1:T(8,128)(2,1)} %copy-done.4, f32[256,304]{0,1:T(8,128)S(1)} %fusion.58), kind=kOutput, calls=%fused_computation.4 | convolution fusion | flops 1117069312 | bytes 10175488 | tf_op jit(solution)/shard_map/dot_general | solution.py:80
  109.6 0.0 reduce-scatter.2.cloned.1.call-update
  109.6 3.3 %constant_dynamic-slice_fusion = f32[64,3584]{0,1:T(8,128)} fusion(f32[256,3584]{0,1:T(8,128)} %copy-done.2, s32[]{:T(128)S(6)} %select_n.68), kind=kLoop, calls=%fused_computation.69 | loop fusion | bytes 1835012 | tf_op jit(solution)/shard_map/dynamic_slice | solution.py:83
  112.9 2.0 %copy.35 = f32[64,3584]{1,0:T(8,128)S(1)} copy(f32[64,3584]{0,1:T(8,128)} %constant_dynamic-slice_fusion) | data formatting | bytes 1835008 | tf_op jit(solution)/shard_map/dynamic_slice | solution.py:83
  115.0 63.1 %reduce-scatter.2.cloned.1.call-done = f32[1,64,3584]{2,1,0:T(8,128)} async-done(((f32[1,256,3584]{2,1,0:T(8,128)}), f32[1,64,3584]{2,1,0:T(8,128)}) %reduce-scatter.2.cloned.1.call-update) | async-done | bytes 917520 | tf_op jit(solution)/shard_map/reduce_scatter | solution.py:81
  178.1 2.0 %fusion.22 = bf16[1,64,3584]{2,1,0:T(8,128)(2,1)} fusion(f32[1,64,3584]{2,1,0:T(8,128)} %reduce-scatter.2.cloned.1.call-done, f32[64,3584]{1,0:T(8,128)S(1)} %copy.35), kind=kLoop, calls=%fused_computation.25 | loop fusion | flops 458752 | bytes 2293760 | tf_op jit(solution)/shard_map/convert_element_type | solution.py:84
  (7 shorter events, 0.0 us)
Async XLA Ops:
  6.5 96.1 %copy-start = (bf16[304,3584]{1,0:T(8,128)(2,1)S(1)}, bf16[304,3584]{1,0:T(8,128)(2,1)}, u32[]{:S(2)}) copy-start(bf16[304,3584]{1,0:T(8,128)(2,1)} %param.19) | copy-start | bytes 6537220
  6.5 19.3 %all-gather.4.cloned.1.call-start = ((), (), s32[]{:S(2)}) async-start(), calls=%async_computation.1 | async-start | bytes 1310720 | tf_op jit(solution)/shard_map/all_gather | solution.py:39
  7.3 36.9 %all-gather.6.cloned.1.call-start = ((), (), s32[]{:S(2)}) async-start(), calls=%async_computation.2 | async-start | bytes 1310720 | tf_op jit(solution)/shard_map/all_gather | solution.py:40
  8.0 83.7 %all-gather.8.cloned.1.call-start = ((), (), s32[]{:S(2)}) async-start(), calls=%async_computation.3 | async-start | bytes 2293760 | tf_op jit(solution)/shard_map/all_gather | solution.py:64
  28.1 2.9 %copy-start.1 = (f32[1024,256,7]{1,0,2:T(8,128)}, f32[1024,256,7]{1,0,2:T(8,128)S(1)}, u32[]{:S(2)}) copy-start(f32[1024,256,7]{1,0,2:T(8,128)S(1)} %get-tuple-element.12) | copy-start | bytes 22020100
  49.4 5.1 %copy-start.5 = (f32[2,3584]{1,0:T(2,128)S(1)}, f32[2,3584]{1,0:T(2,128)}, u32[]{:S(2)}) copy-start(f32[2,3584]{1,0:T(2,128)} %param.16) | copy-start | bytes 86020
  49.4 5.1 %copy-start.7 = (s32[1,8]{1,0:T(1,128)S(1)}, s32[1,8]{1,0:T(1,128)}, u32[]{:S(2)}) copy-start(s32[1,8]{1,0:T(1,128)} %param.14) | copy-start | bytes 100
  50.5 127.6 %reduce-scatter.2.cloned.1.call-start = ((), (), s32[]{:S(2)}) async-start(), calls=%async_computation.4 | async-start | bytes 4587520 | tf_op jit(solution)/shard_map/reduce_scatter | solution.py:81
  95.3 2.1 %copy-start.3 = (bf16[1,256,3584]{1,2,0:T(8,128)(2,1)S(1)}, bf16[1,256,3584]{1,2,0:T(8,128)(2,1)}, u32[]{:S(2)}) copy-start(bf16[1,256,3584]{1,2,0:T(8,128)(2,1)} %copy.27) | copy-start | bytes 5505028
  97.9 4.7 %copy-start.2 = (f32[256,3584]{0,1:T(8,128)}, f32[256,3584]{0,1:T(8,128)S(1)}, u32[]{:S(2)}) copy-start(f32[256,3584]{0,1:T(8,128)S(1)} %get-tuple-element.8) | copy-start | bytes 11010052
  97.9 4.0 %copy-start.6 = (bf16[3584,304]{0,1:T(8,128)(2,1)S(1)}, bf16[3584,304]{0,1:T(8,128)(2,1)}, u32[]{:S(2)}) copy-start(bf16[3584,304]{0,1:T(8,128)(2,1)} %param.17) | copy-start | bytes 6537220
  100.6 1.3 copy-start.4
Sparse Core Ops, SparseCore 0:
  8.9 16.8 all-gather.3
  27.4 16.7 all-gather.5
  50.6 41.1 all-gather.7
  109.7 68.3 reduce-scatter.1
where the time goes:
time: 189 us; the launch traced here: 187 us
  waiting for transfers between devices  126 us (67%)
  local copies, waits for them, and re-layouts  19.9 us (11%)
  matrix products  17.6 us (9%)
  between operations  13.4 us (7%)
  other arithmetic  9.01 us (5%)
    reduce_scatter x1, waiting for transfers between devices, per_device(): lax.psum_scatter(partial_terms[None], 'exp', scatter_dimension=1, tiled=T...  63.1 us
    all_gather x1, waiting for transfers between devices, per_device(): collected = lax.all_gather(own_part[None], 'exp', axis=0, tiled=True)  36.9 us
    all_gather x1, waiting for transfers between devices, per_device(): lax.all_gather(keys, 'ctx', axis=1, tiled=True)  13.6 us
    all_gather x1, waiting for transfers between devices, per_device(): lax.all_gather(values, 'ctx', axis=1, tiled=True)  11.4 us
    unnamed x18, local copies, waits for them, and re-layouts  8.37 us
    dot_general x1, matrix products, per_device(): jnp.dot(hidden, w_down, preferred_element_type=jnp.float32) * keep[:, None]  6.89 us
    dynamic_slice x2, local copies, waits for them, and re-layouts, per_device(): mid_rows = lax.dynamic_slice_in_dim(mid, exp_here * out_rows, out_rows, 0)  5.36 us
    dot_general x1, matrix products, per_device(): jnp.einsum('rqk,kd->rqd', soft, v_head, preferred_element_type=jnp.float32)  5.27 us
  transfers between devices with their start and end apart: 4, of which 4 were waited for; matrix products, arithmetic and copies ran while one was open for 9% of the time, Pallas kernels for 0%

commit v1 on v0

v1 whole, which is shorter than its diff:
```python
import functools

import jax
import jax.numpy as jnp
from jax import lax
from jax.experimental import pallas as pl
from jax.experimental.pallas import tpu as pltpu
from jax.sharding import PartitionSpec as P

KV_HEADS = 4
HEAD_DIM = 128
BLOCK = 128
LANES = 128
MASKED = -1e30
EXP2_SCALE = 1.4426950408889634 / (HEAD_DIM**0.5)
BF16 = jnp.bfloat16
F32 = jnp.float32
OVER_LAST = (((1,), (1,)), ((), ()))
LEAVE, STAY, WHOLE = range(3)
CUTS = 2
WIDE = 128


def fill_bias(bias_ref, mask_ref, labels_ref, here, shards):
    key_in = lax.broadcasted_iota(jnp.int32, (BLOCK, BLOCK), 0)
    query_in = lax.broadcasted_iota(jnp.int32, (BLOCK, BLOCK), 1)
    later = (key_in > query_in).astype(jnp.int32)
    piece_blocks = bias_ref.shape[1] // BLOCK
    any_open = jnp.int32(0)
    for c, shard_of in enumerate(shards):
        for b in range(piece_blocks):
            other = shard_of * piece_blocks + b
            is_open = mask_ref[0, here, other]
            any_open = any_open | is_open
            closed = jnp.where(other == here, 1 - labels_ref[0, here], 0) * later
            closed = jnp.where(is_open == 1, closed, 1)
            bias_ref[c, b * BLOCK : (b + 1) * BLOCK, :] = jnp.where(closed == 1, MASKED, 0.0).astype(BF16)
    return any_open


def attend(q_ref, key_refs, value_refs, bias_ref, s_buf, prior, finish):
    tile, width = q_ref.shape
    group = width // (KV_HEADS * HEAD_DIM)
    rows = group * tile
    row_ids = lax.broadcasted_iota(jnp.int32, (tile, BLOCK), 0)
    col_ids = lax.broadcasted_iota(jnp.int32, (tile, BLOCK), 1)
    picks = jnp.where(row_ids == col_ids, 1.0, 0.0).astype(BF16)
    ones = jnp.ones((key_refs[0].shape[0], HEAD_DIM), BF16)
    limits = {}

    def score(g):
        q_all = jnp.concatenate(
            [
                jnp.concatenate([q_ref[:, (g * group + h) * HEAD_DIM : (g * group + h + 1) * HEAD_DIM], picks], axis=1)
                for h in range(group)
            ],
            axis=0,
        )
        lanes = slice(g * HEAD_DIM, (g + 1) * HEAD_DIM)
        k_all = jnp.concatenate(
            [jnp.concatenate([ref[:, lanes], bias_ref[c]], axis=1) for c, ref in enumerate(key_refs)], axis=0
        )
        s = lax.dot_general(q_all, k_all, OVER_LAST, preferred_element_type=F32)
        s_buf[g % 2] = s
        top = functools.reduce(jnp.maximum, [s[:, n : n + LANES] for n in range(0, s.shape[1], LANES)])
        top = jnp.broadcast_to(jnp.max(top, axis=1, keepdims=True), (rows, LANES))
        if prior is not None:
            top = jnp.maximum(top, prior(g)[2])
        limits[g] = top

    def mix(g):
        lanes = slice(g * HEAD_DIM, (g + 1) * HEAD_DIM)
        shift = limits[g] * EXP2_SCALE
        soft = jnp.concatenate(
            [
                jnp.exp2(s_buf[g % 2, :, n : n + LANES] * EXP2_SCALE - shift).astype(BF16)
                for n in range(0, s_buf.shape[2], LANES)
            ],
            axis=1,
        )
        v_all = jnp.concatenate([jnp.concatenate([ref[:, lanes], ones], axis=1) for ref in value_refs], axis=0)
        mixed = jnp.dot(soft, v_all, preferred_element_type=F32)
        sums, totals = mixed[:, :HEAD_DIM], mixed[:, HEAD_DIM:]
        if prior is not None:
            before = prior(g)
            factor = jnp.exp2((before[2] - limits[g]) * EXP2_SCALE)
            sums = sums + before[0] * factor
            totals = totals + before[1] * factor
        finish(g, sums, totals, limits[g])

    score(0)
    for g in range(KV_HEADS):
        if g + 1 < KV_HEADS:
            score(g + 1)
        mix(g)


def near_kernel(labels_ref, mask_ref, place_ref, q_hbm, *rest):
    pieces = (len(rest) - 7) // 2
    key_refs, value_refs = rest[:pieces], rest[pieces : 2 * pieces]
    sums_ref, totals_ref, limits_ref, q_ref, bias_buf, s_buf, sem = rest[2 * pieces :]
    blocks, tile, _ = q_ref.shape
    ctx_here, section = place_ref[0], place_ref[1]

    loads = [pltpu.make_async_copy(q_hbm.at[pl.ds(t * tile, tile)], q_ref.at[t], sem.at[t]) for t in range(blocks)]
    for copy in loads:
        copy.start()
    for t in range(blocks):
        fill_bias(bias_buf.at[t], mask_ref, labels_ref, ctx_here * blocks + t, [ctx_here ^ c for c in range(pieces)])
    for copy in loads:
        copy.wait()

    def block_of(t, carry):
        @pl.when(labels_ref[0, ctx_here * blocks + t] == section)
        def _():
            def finish(g, sums, totals, limit):
                sums_ref[t, g] = sums
                totals_ref[t, g] = totals
                limits_ref[t, g] = limit

            attend(q_ref.at[t], key_refs, value_refs, bias_buf.at[t], s_buf, None, finish)

        return carry

    lax.fori_loop(0, blocks, block_of, 0)


def far_kernel(
    mode, first_piece, waited, labels_ref, mask_ref, place_ref, q_ref, res_hbm, gains_ref, sums_ref, totals_ref,
    limits_ref, *rest,
):
    rest = rest[waited:]
    outs = {LEAVE: 2 * CUTS, STAY: 2, WHOLE: 1}[mode]
    pieces = (len(rest) - outs - 13) // 2
    key_refs, value_refs = rest[:pieces], rest[pieces : 2 * pieces]
    wg_hbm, wu_hbm, wd_hbm = rest[2 * pieces : 2 * pieces + 3]
    out_refs = rest[2 * pieces + 3 : 2 * pieces + 3 + outs]
    res_buf, w_buf, wd_buf, bias_buf, s_buf, att_buf, norm_buf, hid_buf, sem, w_sem = rest[2 * pieces + 3 + outs :]
    blocks, tile, width = q_ref.shape
    units = wg_hbm.shape[0]
    up_at = w_buf.shape[0] - units
    group = width // (KV_HEADS * HEAD_DIM)
    ctx_here, section, low, first = place_ref[0], place_ref[1], place_ref[2], place_ref[4]
    chosen = {LEAVE: [1 - section], STAY: [section], WHOLE: list(range(blocks))}[mode]

    loads = []
    for i, t in enumerate(chosen):
        rows = pl.ds(pl.multiple_of(t * tile, tile), tile)
        loads.append(pltpu.make_async_copy(res_hbm.at[rows], res_buf.at[pl.ds(i * tile, tile)], sem.at[i]))
    loads.append(pltpu.make_async_copy(wg_hbm, w_buf.at[pl.ds(0, units)], w_sem.at[0]))
    loads.append(pltpu.make_async_copy(wu_hbm, w_buf.at[pl.ds(up_at, units)], w_sem.at[1]))
    later = pltpu.make_async_copy(wd_hbm, wd_buf, w_sem.at[2])
    for copy in loads:
        copy.start()
    later.start()

    matches = [labels_ref[0, ctx_here * blocks + t] == section for t in chosen]
    for i, t in enumerate(chosen):
        opened = fill_bias(
            bias_buf, mask_ref, labels_ref, ctx_here * blocks + t,
            [ctx_here ^ (first_piece + c) for c in range(pieces)],
        )

        def finish(g, sums, totals, _):
            attended = (sums / totals).astype(BF16)
            for h in range(group):
                at = (g * group + h) * HEAD_DIM
                att_buf[i * tile : (i + 1) * tile, at : at + HEAD_DIM] = attended[h * tile : (h + 1) * tile]

        def prior(g):
            return sums_ref[t, g], totals_ref[t, g], limits_ref[t, g]

        @pl.when(matches[i] & (opened > 0))
        def _():
            attend(q_ref.at[t], key_refs, value_refs, bias_buf, s_buf, prior, finish)

        @pl.when(matches[i] & (opened == 0))
        def _():
            for g in range(KV_HEADS):
                finish(g, sums_ref[t, g], totals_ref[t, g], None)

        @pl.when(jnp.logical_not(matches[i]))
        def _():
            norm_buf[i * tile : (i + 1) * tile, :] = jnp.zeros((tile, width), BF16)

    for copy in loads:
        copy.wait()

    step = 16
    for i in range(len(chosen)):

        @pl.when(matches[i])
        def _():
            gain = gains_ref[pl.ds(section, 1), :]

            def norm_rows(j, carry):
                rows = pl.ds(pl.multiple_of(i * tile + j * step, step), step)
                mid = res_buf[rows, :].astype(F32) + att_buf[rows, :].astype(F32)
                factor = lax.rsqrt(jnp.mean(mid * mid, axis=-1, keepdims=True) + 1e-05)
                norm_buf[rows, :] = (mid * factor * gain).astype(BF16)
                return carry

            lax.fori_loop(0, tile // step, norm_rows, 0)

    later.wait()
    half = tile // 2
    own = pl.ds(pl.multiple_of(low * half, half), half)
    other = pl.ds(pl.multiple_of(half - low * half, half), half)

    def mid_of(rows, cols):
        return res_buf[rows, cols].astype(F32) + att_buf[rows, cols].astype(F32)

    @pl.when(functools.reduce(jnp.logical_or, matches))
    def _():
        both = lax.dot_general(norm_buf[...], w_buf[...], OVER_LAST, preferred_element_type=F32)
        gate, upper = both[:, :units], both[:, up_at : up_at + units]
        hid_buf[...] = (gate * upper / (1.0 + jnp.exp(-gate))).astype(BF16)
        if mode == LEAVE:
            left = jnp.concatenate([hid_buf[own, :], hid_buf[other, :]], axis=0)
        elif mode == STAY:
            left = hid_buf[own, :]
            out_refs[1][...] = hid_buf[other, :]
        else:
            left = hid_buf[...]
        cut = width // CUTS
        for n in range(0, width, WIDE):
            cols = slice(n, n + WIDE)
            terms = jnp.dot(left, wd_buf[:, cols], preferred_element_type=F32)
            if mode == LEAVE:
                at = slice(n % cut, n % cut + WIDE)
                out_refs[n // cut][:, at] = terms[:half] + mid_of(own, cols)
                out_refs[CUTS + n // cut][:, at] = terms[half:].astype(BF16)
            elif mode == STAY:
                out_refs[0][:, cols] = terms + mid_of(own, cols)
            else:
                for i in range(len(chosen)):
                    span = slice(i * tile, (i + 1) * tile)
                    kept = terms[span] + mid_of(span, cols) * first.astype(F32)
                    out_refs[0][span, cols] = jnp.where(matches[i], kept, 0.0)

    @pl.when(jnp.logical_not(functools.reduce(jnp.logical_or, matches)))
    def _():
        for ref in out_refs:
            ref[...] = jnp.zeros(ref.shape, ref.dtype)


def down_kernel(labels_ref, place_ref, in_ref, base_ref, *rest):
    quarter_refs, out_ref = rest[:-1], rest[-1]
    cut = quarter_refs[0].shape[1]
    ctx_here, section, core, row = place_ref[0], place_ref[1], place_ref[3], place_ref[5]
    match = labels_ref[0, ctx_here * 2 + section] == section
    here = 2 * row + core

    @pl.when(match)
    def _():
        for i, ref in enumerate(quarter_refs):
            for n in range(0, cut, LANES):
                wide = min(WIDE, cut - n)
                if n % WIDE:
                    continue
                cols = pl.ds(pl.multiple_of((here ^ i) * cut + n, LANES), wide)
                terms = jnp.dot(in_ref[...], ref[:, n : n + wide], preferred_element_type=F32)
                out_ref[:, cols] = terms + base_ref[:, cols]

    @pl.when(jnp.logical_not(match))
    def _():
        out_ref[...] = jnp.zeros(out_ref.shape, out_ref.dtype)


SMEM = pl.BlockSpec(memory_space=pltpu.SMEM)
HBM = pl.BlockSpec(memory_space=pltpu.HBM)
VMEM = pl.BlockSpec(memory_space=pltpu.VMEM)


def params(mib):
    return pltpu.CompilerParams(vmem_limit_bytes=mib * 1024 * 1024)


def stay(array):
    return pltpu.with_memory_space_constraint(array, pltpu.HBM)


def cost(flops, moved, powers=0):
    return pl.CostEstimate(flops=flops, bytes_accessed=moved, transcendentals=powers)


def near_attention(labels, mask, place, queries, keys, values):
    shard, width = queries.shape
    blocks = shard // BLOCK
    pieces = len(keys)
    piece_rows = keys[0].shape[0]
    rows = width // (KV_HEADS * HEAD_DIM) * BLOCK
    count = piece_rows * pieces
    state = jax.ShapeDtypeStruct((blocks, KV_HEADS, rows, LANES), F32)
    return pl.pallas_call(
        near_kernel,
        out_shape=[state, state, state, jax.ShapeDtypeStruct((blocks, BLOCK, width), BF16)],
        in_specs=[SMEM, SMEM, SMEM, HBM] + [VMEM] * (2 * pieces),
        out_specs=[VMEM] * 4,
        scratch_shapes=[
            pltpu.VMEM((blocks, pieces, piece_rows, BLOCK), BF16),
            pltpu.VMEM((2, rows, count), F32),
            pltpu.SemaphoreType.DMA((blocks,)),
        ],
        compiler_params=params(24),
        cost_estimate=cost(800 * shard * width * count, 2 * shard * width, shard * width // HEAD_DIM * count),
    )(labels, mask, place, queries, *keys, *values)


def far_attention(mode, first_piece, labels, mask, place, queries, residual, gains, state, keys, values, wg, wu, wd, after=()):
    blocks, tile, width = queries.shape
    pieces = len(keys)
    piece_rows = keys[0].shape[0]
    rows = width // (KV_HEADS * HEAD_DIM) * BLOCK
    count = piece_rows * pieces
    units = wg.shape[0]
    up_at = -(-units // LANES) * LANES
    taken = tile * (blocks if mode == WHOLE else 1)
    shape = jax.ShapeDtypeStruct
    outs = {
        LEAVE: [shape((tile // 2, width // CUTS), kind) for kind in (F32, BF16) for _ in range(CUTS)],
        STAY: [shape((tile // 2, width), F32), shape((tile // 2, units), BF16)],
        WHOLE: [shape((taken, width), F32)],
    }[mode]
    return pl.pallas_call(
        functools.partial(far_kernel, mode, first_piece, len(after)),
        out_shape=outs,
        in_specs=[SMEM, SMEM, SMEM, VMEM, HBM, VMEM] + [VMEM] * 3 + [pl.BlockSpec(memory_space=pl.ANY)] * len(after) + [VMEM] * (2 * pieces) + [HBM] * 3,
        out_specs=[VMEM] * len(outs),
        scratch_shapes=[
            pltpu.VMEM((taken, width), BF16),
            pltpu.VMEM((up_at + units, width), BF16),
            pltpu.VMEM(wd.shape, BF16),
            pltpu.VMEM((pieces, piece_rows, BLOCK), BF16),
            pltpu.VMEM((2, rows, count), F32),
            pltpu.VMEM((taken, width), BF16),
            pltpu.VMEM((taken, width), BF16),
            pltpu.VMEM((taken, units), BF16),
            pltpu.SemaphoreType.DMA((blocks,)),
            pltpu.SemaphoreType.DMA((3,)),
        ],
        compiler_params=params(30),
        cost_estimate=cost(
            (800 if mode == STAY else 1) * taken * width * count, width * units, taken * count
        ),
    )(labels, mask, place, queries, residual, gains, *state, *after, *keys, *values, wg, wu, wd)


def down_rest(labels, place, arrived, base, quarters):
    rows, width = base.shape
    units = arrived.shape[1]
    return pl.pallas_call(
        down_kernel,
        out_shape=jax.ShapeDtypeStruct((rows, width), F32),
        in_specs=[SMEM, SMEM] + [VMEM] * (2 + len(quarters)),
        out_specs=VMEM,
        compiler_params=params(16),
        cost_estimate=cost(rows * units, rows * units),
    )(labels, place, arrived, base, *quarters)


def xor_pairs(count, bits):
    return [(i, i ^ bits) for i in range(count)]


def per_device(queries, keys, values, residual, labels, block_mask, gains, w_gate, w_up, w_down):
    shard, width = queries.shape[1:]
    exp_count = lax.axis_size("exp")
    exp_here = lax.axis_index("exp")
    ctx_count = lax.axis_size("ctx")
    ctx_here = lax.axis_index("ctx")
    half = exp_count // 2
    split = exp_count == 4 and shard == 2 * BLOCK and ctx_count == 4 and lax.axis_size("dp") == 2
    section = exp_here // half
    low = exp_here % 2 if split else jnp.zeros_like(exp_here)
    core = ctx_here % 2
    first = exp_here % half == 0
    row = lax.axis_index("dp") % 2
    place = jnp.stack([value.astype(jnp.int32) for value in (ctx_here, section, low, core, first, row)])
    labels, block_mask, gains = stay(labels), stay(block_mask), stay(gains)
    own_q, own_res = stay(queries[0]), stay(residual[0])

    held = {0: (keys[0], values[0])}

    def spread(bits):
        pairs = xor_pairs(ctx_count, bits)
        for at, (k, v) in list(held.items()):
            held[at ^ bits] = (lax.ppermute(k, "ctx", pairs), lax.ppermute(v, "ctx", pairs))

    def swap(array):
        return lax.ppermute(array, "ctx", xor_pairs(ctx_count, 1))

    bits = ctx_count // 2
    while bits > 1:
        spread(bits)
        bits //= 2
    held[1] = (swap(keys[0]), swap(values[0]))
    *state, own_q = near_attention(
        labels, block_mask, place, own_q, [keys[0], held[1][0]], [values[0], held[1][1]]
    )
    if split:
        z_pairs = xor_pairs(exp_count, 1)
        cut = width // 4
        piece = lax.dynamic_slice_in_dim(w_down, (2 * row + core) * cut, cut, 1)
        quarter = lax.ppermute(piece, "exp", z_pairs)
    for at in range(2, ctx_count, 2):
        k, v = held[at]
        k, v, *state = lax.optimization_barrier((k, v, *state))
        held[at] = (k, v)
        held[at + 1] = (swap(k), swap(v))
    far = range(2, ctx_count)
    far_keys, far_values = [held[c][0] for c in far], [held[c][1] for c in far]
    shared = (labels, block_mask, place, own_q, own_res, gains)
    weights = (far_keys, far_values, stay(w_gate.T), stay(w_up.T), stay(w_down))
    if not split:
        (terms,) = far_attention(WHOLE, 2, *shared, state, *weights)
        return lax.psum_scatter(terms[None], "exp", scatter_dimension=1, tiled=True).astype(BF16)

    made = far_attention(LEAVE, 2, *shared, state, *weights)
    own_terms, sent = made[:CUTS], made[CUTS:]
    arrived = [lax.ppermute(part, "exp", z_pairs) for part in sent]
    leaving = [(mine + part.astype(F32)).astype(BF16) for mine, part in zip(own_terms, arrived)]
    crossed = [lax.ppermute(part, "exp", xor_pairs(exp_count, 2)) for part in leaving]

    quarter, _ = lax.optimization_barrier((quarter, sent[-1]))
    beside = lax.ppermute(quarter, "dp", xor_pairs(2, 1))
    quarters = [quarter, swap(quarter), beside, swap(beside)]
    base, send = far_attention(STAY, 2, *shared, state, *weights, after=leaving)
    staying = down_rest(labels, place, lax.ppermute(send, "exp", z_pairs), base, quarters)
    return (staying + jnp.concatenate(crossed, axis=1).astype(F32)).astype(BF16)[None]


def solution(mesh):
    placed = (
        P("dp", "ctx", None),
        P("dp", "ctx", None),
        P("dp", "ctx", None),
        P("dp", "ctx", None),
        P("dp", None),
        P("dp", None, None),
        P(),
        P(None, "exp"),
        P(None, "exp"),
        P("exp", None),
    )
    return jax.shard_map(
        per_device,
        mesh=mesh,
        in_specs=placed,
        out_specs=P("dp", ("ctx", "exp"), None),
        check_vma=False,
    )
```

time: 189 us -> 63.7 us (0.34)
  the two profiles are of different devices: /device:TPU:14 before, /device:TPU:0 now
where the time goes in v1:
time: 63.7 us; the launch traced here: 63.4 us
  starting transfers between devices  27.8 us (44%)
  waiting for transfers between devices  15.8 us (25%)
  Pallas kernels  12.4 us (19%)
  local copies, waits for them, and re-layouts  3.89 us (6%)
  other arithmetic  3.39 us (5%)
    ppermute x2, starting transfers between devices, per_device(): lax.ppermute(part, 'exp', xor_pairs(exp_count, 2))  12.8 us
    ppermute x1, waiting for transfers between devices, per_device(): lax.ppermute(send, 'exp', z_pairs)  10 us
    pallas_call x2, Pallas kernels, far_attention(): pl.pallas_call(functools.partial(far_kernel, mode, first_piece, len(after...  8.6 us
    ppermute x6, starting transfers between devices, swap(): return lax.ppermute(array, 'ctx', xor_pairs(ctx_count, 1))  5 us
    ppermute x1, waiting for transfers between devices, spread(): lax.ppermute(v, 'ctx', pairs)  4.19 us
    ppermute x1, starting transfers between devices, spread(): lax.ppermute(k, 'ctx', pairs)  2.97 us
    pallas_call x1, Pallas kernels, near_attention(): pl.pallas_call(near_kernel, out_shape=[state, state, state, jax.ShapeDtyp...  2.21 us
    ppermute x2, starting transfers between devices, per_device(): arrived = [lax.ppermute(part, 'exp', z_pairs) for part in sent]  2.09 us
  transfers between devices with their start and end apart: 15, of which 4 were waited for; matrix products, arithmetic and copies ran while one was open for 5% of the time, Pallas kernels for 20%

profile of v1, /device:TPU:0, one launch (start us, length us, event | category | flops | bytes accessed | tf_op | source)
XLA Modules:
  0.0 63.4 jit_solution(15417370222277684211)
XLA Ops:
  0.0 0.5 collective-permute-start
  0.5 0.1 collective-permute-start.1
  0.5 3.0 %collective-permute-start.2 = (bf16[256,512]{1,0:T(8,128)(2,1)}, bf16[256,512]{1,0:T(8,128)(2,1)}, u32[]{:S(2)}, u32[]{:S(2)}) collective-permute-start(bf16[256,512]{1,0:T(8,128)(2,1)} %bitcast.15), channel_id=1, source_target_pairs={{0,8},{4,12},{8,0},{12,4},{1,9},{5,13},{9,1},{13,5},{2,10},{6,14},... | collective-permute-start | bytes 786440 | tf_op jit(solution)/shard_map/ppermute | solution.py:388
  3.5 0.0 collective-permute-start.3
  3.5 1.9 %constant_dynamic-slice_fusion = bf16[304,896]{1,0:T(8,128)(2,1)} fusion(bf16[304,3584]{1,0:T(8,128)(2,1)} %rest_8_.1, s32[]{:T(128)S(6)} %select_n.28), kind=kLoop, calls=%fused_computation.4 | loop fusion | bytes 1089540 | tf_op jit(solution)/shard_map/dynamic_slice | solution.py:404
  5.4 2.0 %collective-permute-start.9 = (bf16[304,896]{1,0:T(8,128)(2,1)}, bf16[304,896]{1,0:T(8,128)(2,1)}, u32[]{:S(2)}, u32[]{:S(2)}) collective-permute-start(bf16[304,896]{1,0:T(8,128)(2,1)} %constant_dynamic-slice_fusion), channel_id=1, source_target_pairs={{0,1},{1,0},{2,3},{3,2},{4,5},{5,4},{6,7},{7,6},{8,9},{9,8},{10,11... | collective-permute-start | bytes 1634312 | tf_op jit(solution)/shard_map/ppermute | solution.py:405
  7.5 0.1 stack.31.place_ref
  7.6 0.0 collective-permute-done.rest_1_
  7.6 0.0 collective-permute-done.1.rest_3_
  7.6 0.0 copy-start
  7.6 0.9 %copy-done = bf16[1,256,512]{2,1,0:T(8,128)(2,1)S(1)} copy-done((bf16[1,256,512]{2,1,0:T(8,128)(2,1)S(1)}, bf16[1,256,512]{2,1,0:T(8,128)(2,1)}, u32[]{:S(2)}) %copy-start) | copy-done | bytes 262168
  8.5 0.0 copy-start.1
  8.5 0.9 %copy-done.1 = bf16[1,256,512]{2,1,0:T(8,128)(2,1)S(1)} copy-done((bf16[1,256,512]{2,1,0:T(8,128)(2,1)S(1)}, bf16[1,256,512]{2,1,0:T(8,128)(2,1)}, u32[]{:S(2)}) %copy-start.1) | copy-done | bytes 262168
  9.5 2.2 %shard_map.100 = (f32[2,4,896,128]{3,2,1,0:T(8,128)S(1)}, f32[2,4,896,128]{3,2,1,0:T(8,128)S(1)}, f32[2,4,896,128]{3,2,1,0:T(8,128)S(1)}, bf16[2,128,3584]{2,1,0:T(8,128)(2,1)S(1)}) custom-call(s32[1,8]{1,0:T(1,128)} %labels_ref.7, s32[1,8,8]{2,1,0:T(8,128)} %mask_ref.5, s32[6]{0:T(128)S(1)} %stack.31.place_ref, bf16[256,3584]{1,0:T(8,128)(2,1)} %bitcast.26, ...), custom_call_target="tpu_custom_call" | custom-call | flops 375809638400 | bytes 1835008 | tf_op jit(solution)/shard_map/pallas_call | solution.py:295
  11.7 0.0 collective-permute-done.2.rest_0_.rest_2_
  11.7 4.2 %collective-permute-done.3.rest_2_.rest_4_ = bf16[256,512]{1,0:T(8,128)(2,1)} collective-permute-done((bf16[256,512]{1,0:T(8,128)(2,1)}, bf16[256,512]{1,0:T(8,128)(2,1)}, u32[]{:S(2)}, u32[]{:S(2)}) %collective-permute-start.3) | collective-permute-done | bytes 262176 | tf_op jit(solution)/shard_map/ppermute | solution.py:388
  15.9 0.0 collective-permute-start.4
  15.9 0.5 collective-permute-start.5
  16.4 1.2 %collective-permute-done.4.rest_1_.rest_3_ = bf16[256,512]{1,0:T(8,128)(2,1)S(1)} collective-permute-done((bf16[256,512]{1,0:T(8,128)(2,1)}, bf16[256,512]{1,0:T(8,128)(2,1)S(1)}, u32[]{:S(2)}, u32[]{:S(2)}) %collective-permute-start.4) | collective-permute-done | bytes 262176 | tf_op jit(solution)/shard_map/ppermute | solution.py:391
  17.6 0.4 collective-permute-done.5.rest_3_.rest_5_
  18.0 4.3 %shard_map.101 = (f32[64,1792]{1,0:T(8,128)S(1)}, f32[64,1792]{1,0:T(8,128)S(1)}, bf16[64,1792]{1,0:T(8,128)(2,1)S(1)}, bf16[64,1792]{1,0:T(8,128)(2,1)S(1)}) custom-call(s32[1,8]{1,0:T(1,128)} %labels_ref.7, s32[1,8,8]{2,1,0:T(8,128)} %mask_ref.5, s32[6]{0:T(128)S(1)} %stack.31.place_ref, bf16[2,128,3584]{2,1,0:T(8,128)(2,1)S(1)} %get-tuple-element.21.q_ref, ...), custom_call_target="tpu_custom_call" | custom-call | flops 234881024 | bytes 1089536 | tf_op jit(solution)/shard_map/pallas_call | solution.py:325
  22.3 1.9 %collective-permute-start.7 = (bf16[64,1792]{1,0:T(8,128)(2,1)S(1)}, bf16[64,1792]{1,0:T(8,128)(2,1)S(1)}, u32[]{:S(2)}, u32[]{:S(2)}) collective-permute-start(bf16[64,1792]{1,0:T(8,128)(2,1)S(1)} %get-tuple-element.33), channel_id=1, source_target_pairs={{0,1},{1,0},{2,3},{3,2},{4,5},{5,4},{6,7},{7,6},{8,9},{9,8},{10,11... | collective-permute-start | bytes 688136 | tf_op jit(solution)/shard_map/ppermute | solution.py:421
  24.2 0.2 collective-permute-start.6
  24.4 0.0 collective-permute-done.9.rest_0_
  24.4 4.0 %collective-permute-start.10 = (bf16[304,896]{1,0:T(8,128)(2,1)}, bf16[304,896]{1,0:T(8,128)(2,1)}, u32[]{:S(2)}, u32[]{:S(2)}) collective-permute-start(bf16[304,896]{1,0:T(8,128)(2,1)} %collective-permute-done.9.rest_0_), channel_id=1, source_target_pairs={{0,4},{4,0},{8,12},{12,8},{1,5},{5,1},{9,13},{13,9},{2,6},{6,2},{1... | collective-permute-start | bytes 1634312 | tf_op jit(solution)/shard_map/ppermute | solution.py:391
  28.4 2.0 %collective-permute-start.11 = (bf16[304,896]{1,0:T(8,128)(2,1)}, bf16[304,896]{1,0:T(8,128)(2,1)}, u32[]{:S(2)}, u32[]{:S(2)}) collective-permute-start(bf16[304,896]{1,0:T(8,128)(2,1)} %collective-permute-done.9.rest_0_), channel_id=1, source_target_pairs={{0,16},{16,0},{1,17},{17,1},{2,18},{18,2},{3,19},{19,3},{4,20},{20... | collective-permute-start | bytes 1634312 | tf_op jit(solution)/shard_map/ppermute | solution.py:426
  30.4 0.0 collective-permute-done.7
  30.4 0.7 %add_convert_fusion.1.rest_1_ = bf16[64,1792]{1,0:T(8,128)(2,1)} fusion(f32[64,1792]{1,0:T(8,128)S(1)} %get-tuple-element.32, bf16[64,1792]{1,0:T(8,128)(2,1)S(1)} %collective-permute-done.7), kind=kLoop, calls=%fused_computation.2 | loop fusion | flops 344064 | bytes 917504 | tf_op jit(solution)/shard_map/convert_element_type | solution.py:422
  31.1 8.7 %collective-permute-start.14 = (bf16[64,1792]{1,0:T(8,128)(2,1)}, bf16[64,1792]{1,0:T(8,128)(2,1)}, u32[]{:S(2)}, u32[]{:S(2)}) collective-permute-start(bf16[64,1792]{1,0:T(8,128)(2,1)} %add_convert_fusion.1.rest_1_), channel_id=1, source_target_pairs={{0,2},{1,3},{2,0},{3,1},{4,6},{5,7},{6,4},{7,5},{8,10},{9,11},{10,... | collective-permute-start | bytes 688136 | tf_op jit(solution)/shard_map/ppermute | solution.py:423
  39.8 0.0 collective-permute-done.6
  39.8 0.7 %add_convert_fusion.2.rest_0_ = bf16[64,1792]{1,0:T(8,128)(2,1)} fusion(f32[64,1792]{1,0:T(8,128)S(1)} %get-tuple-element.30, bf16[64,1792]{1,0:T(8,128)(2,1)S(1)} %collective-permute-done.6), kind=kLoop, calls=%fused_computation.3 | loop fusion | flops 344064 | bytes 917504 | tf_op jit(solution)/shard_map/convert_element_type | solution.py:422
  40.5 4.2 %collective-permute-start.13 = (bf16[64,1792]{1,0:T(8,128)(2,1)}, bf16[64,1792]{1,0:T(8,128)(2,1)}, u32[]{:S(2)}, u32[]{:S(2)}) collective-permute-start(bf16[64,1792]{1,0:T(8,128)(2,1)} %add_convert_fusion.2.rest_0_), channel_id=1, source_target_pairs={{0,2},{1,3},{2,0},{3,1},{4,6},{5,7},{6,4},{7,5},{8,10},{9,11},{10,... | collective-permute-start | bytes 688136 | tf_op jit(solution)/shard_map/ppermute | solution.py:423
  44.7 0.0 collective-permute-done.11.rest_2_
  44.7 0.0 collective-permute-start.12
  44.7 4.3 %shard_map.102 = (f32[64,3584]{1,0:T(8,128)S(1)}, bf16[64,304]{1,0:T(8,128)(2,1)S(1)}) custom-call(s32[1,8]{1,0:T(1,128)} %labels_ref.7, s32[1,8,8]{2,1,0:T(8,128)} %mask_ref.5, s32[6]{0:T(128)S(1)} %stack.31.place_ref, bf16[2,128,3584]{2,1,0:T(8,128)(2,1)S(1)} %get-tuple-element.21.q_ref, bf16[256,3584]{1,0:T(8,128)(2,1)} %bitcast.25, f32[2,3584]{1,0:T(2,128)} %gains_ref.3, ...), custom_call_target="tpu_custom_call" | custom-call | flops 187904819200 | bytes 1089536 | tf_op jit(solution)/shard_map/pallas_call | solution.py:325
  49.0 0.8 %collective-permute-start.8 = (bf16[64,304]{1,0:T(8,128)(2,1)S(1)}, bf16[64,304]{1,0:T(8,128)(2,1)S(1)}, u32[]{:S(2)}, u32[]{:S(2)}) collective-permute-start(bf16[64,304]{1,0:T(8,128)(2,1)S(1)} %get-tuple-element.34), channel_id=1, source_target_pairs={{0,1},{1,0},{2,3},{3,2},{4,5},{5,4},{6,7},{7,6},{8,9},{9,8},{10,11... | collective-permute-start | bytes 116744 | tf_op jit(solution)/shard_map/ppermute | solution.py:429
  49.8 10.0 %collective-permute-done.8.in_ref = bf16[64,304]{1,0:T(8,128)(2,1)S(1)} collective-permute-done((bf16[64,304]{1,0:T(8,128)(2,1)S(1)}, bf16[64,304]{1,0:T(8,128)(2,1)S(1)}, u32[]{:S(2)}, u32[]{:S(2)}) %collective-permute-start.8) | collective-permute-done | bytes 38944 | tf_op jit(solution)/shard_map/ppermute | solution.py:429
  59.8 0.0 collective-permute-done.10.rest_1_
  59.8 0.0 collective-permute-done.12.rest_3_
  59.8 1.6 %shard_map.103 = f32[64,3584]{1,0:T(8,128)S(1)} custom-call(s32[1,8]{1,0:T(1,128)} %labels_ref.7, s32[6]{0:T(128)S(1)} %stack.31.place_ref, bf16[64,304]{1,0:T(8,128)(2,1)S(1)} %collective-permute-done.8.in_ref, f32[64,3584]{1,0:T(8,128)S(1)} %get-tuple-element.35.base_ref, bf16[304,896]{1,0:T(8,128)(2,1)} %collective-permute-done.9.rest_0_, ...), custom_call_target="tpu_custom_call" | custom-call | flops 19456 | bytes 19456 | tf_op jit(solution)/shard_map/pallas_call | solution.py:352
  61.5 0.0 collective-permute-done.14
  61.5 0.0 collective-permute-done.13
  61.5 1.9 %fusion = bf16[1,64,3584]{2,1,0:T(8,128)(2,1)} fusion(f32[64,3584]{1,0:T(8,128)S(1)} %shard_map.103, bf16[64,1792]{1,0:T(8,128)(2,1)} %collective-permute-done.14, bf16[64,1792]{1,0:T(8,128)(2,1)} %collective-permute-done.13), kind=kLoop, calls=%fused_computation.1 | loop fusion | flops 1376256 | bytes 1835008 | tf_op jit(solution)/shard_map/broadcast_in_dim | solution.py:430
Async XLA Ops:
  0.0 7.6 %collective-permute-start = (bf16[256,512]{1,0:T(8,128)(2,1)}, bf16[256,512]{1,0:T(8,128)(2,1)S(1)}, u32[]{:S(2)}, u32[]{:S(2)}) collective-permute-start(bf16[256,512]{1,0:T(8,128)(2,1)} %bitcast.14), channel_id=1, source_target_pairs={{0,4},{4,0},{8,12},{12,8},{1,5},{5,1},{9,13},{13,9},{2,6},{6,2},{1... | collective-permute-start | bytes 786440 | tf_op jit(solution)/shard_map/ppermute | solution.py:391
  0.5 7.1 %collective-permute-start.1 = (bf16[256,512]{1,0:T(8,128)(2,1)}, bf16[256,512]{1,0:T(8,128)(2,1)S(1)}, u32[]{:S(2)}, u32[]{:S(2)}) collective-permute-start(bf16[256,512]{1,0:T(8,128)(2,1)} %bitcast.17), channel_id=1, source_target_pairs={{0,4},{4,0},{8,12},{12,8},{1,5},{5,1},{9,13},{13,9},{2,6},{6,2},{1... | collective-permute-start | bytes 786440 | tf_op jit(solution)/shard_map/ppermute | solution.py:391
  0.5 11.2 %collective-permute-start.2 = (bf16[256,512]{1,0:T(8,128)(2,1)}, bf16[256,512]{1,0:T(8,128)(2,1)}, u32[]{:S(2)}, u32[]{:S(2)}) collective-permute-start(bf16[256,512]{1,0:T(8,128)(2,1)} %bitcast.15), channel_id=1, source_target_pairs={{0,8},{4,12},{8,0},{12,4},{1,9},{5,13},{9,1},{13,5},{2,10},{6,14},... | collective-permute-start | bytes 786440 | tf_op jit(solution)/shard_map/ppermute | solution.py:388
  3.5 12.4 %collective-permute-start.3 = (bf16[256,512]{1,0:T(8,128)(2,1)}, bf16[256,512]{1,0:T(8,128)(2,1)}, u32[]{:S(2)}, u32[]{:S(2)}) collective-permute-start(bf16[256,512]{1,0:T(8,128)(2,1)} %bitcast.18), channel_id=1, source_target_pairs={{0,8},{4,12},{8,0},{12,4},{1,9},{5,13},{9,1},{13,5},{2,10},{6,14},... | collective-permute-start | bytes 786440 | tf_op jit(solution)/shard_map/ppermute | solution.py:388
  5.4 19.0 %collective-permute-start.9 = (bf16[304,896]{1,0:T(8,128)(2,1)}, bf16[304,896]{1,0:T(8,128)(2,1)}, u32[]{:S(2)}, u32[]{:S(2)}) collective-permute-start(bf16[304,896]{1,0:T(8,128)(2,1)} %constant_dynamic-slice_fusion), channel_id=1, source_target_pairs={{0,1},{1,0},{2,3},{3,2},{4,5},{5,4},{6,7},{7,6},{8,9},{9,8},{10,11... | collective-permute-start | bytes 1634312 | tf_op jit(solution)/shard_map/ppermute | solution.py:405
  7.6 1.0 %copy-start = (bf16[1,256,512]{2,1,0:T(8,128)(2,1)S(1)}, bf16[1,256,512]{2,1,0:T(8,128)(2,1)}, u32[]{:S(2)}) copy-start(bf16[1,256,512]{2,1,0:T(8,128)(2,1)} %param.11) | copy-start | bytes 786436
  8.5 0.9 %copy-start.1 = (bf16[1,256,512]{2,1,0:T(8,128)(2,1)S(1)}, bf16[1,256,512]{2,1,0:T(8,128)(2,1)}, u32[]{:S(2)}) copy-start(bf16[1,256,512]{2,1,0:T(8,128)(2,1)} %param.12) | copy-start | bytes 786436
  15.9 1.7 %collective-permute-start.4 = (bf16[256,512]{1,0:T(8,128)(2,1)}, bf16[256,512]{1,0:T(8,128)(2,1)S(1)}, u32[]{:S(2)}, u32[]{:S(2)}) collective-permute-start(bf16[256,512]{1,0:T(8,128)(2,1)} %collective-permute-done.2.rest_0_.rest_2_), channel_id=1, source_target_pairs={{0,4},{4,0},{8,12},{12,8},{1,5},{5,1},{9,13},{13,9},{2,6},{6,2},{1... | collective-permute-start | bytes 786440 | tf_op jit(solution)/shard_map/ppermute | solution.py:391
  15.9 2.1 %collective-permute-start.5 = (bf16[256,512]{1,0:T(8,128)(2,1)}, bf16[256,512]{1,0:T(8,128)(2,1)S(1)}, u32[]{:S(2)}, u32[]{:S(2)}) collective-permute-start(bf16[256,512]{1,0:T(8,128)(2,1)} %collective-permute-done.3.rest_2_.rest_4_), channel_id=1, source_target_pairs={{0,4},{4,0},{8,12},{12,8},{1,5},{5,1},{9,13},{13,9},{2,6},{6,2},{1... | collective-permute-start | bytes 786440 | tf_op jit(solution)/shard_map/ppermute | solution.py:391
  22.3 8.1 %collective-permute-start.7 = (bf16[64,1792]{1,0:T(8,128)(2,1)S(1)}, bf16[64,1792]{1,0:T(8,128)(2,1)S(1)}, u32[]{:S(2)}, u32[]{:S(2)}) collective-permute-start(bf16[64,1792]{1,0:T(8,128)(2,1)S(1)} %get-tuple-element.33), channel_id=1, source_target_pairs={{0,1},{1,0},{2,3},{3,2},{4,5},{5,4},{6,7},{7,6},{8,9},{9,8},{10,11... | collective-permute-start | bytes 688136 | tf_op jit(solution)/shard_map/ppermute | solution.py:421
  24.2 15.6 %collective-permute-start.6 = (bf16[64,1792]{1,0:T(8,128)(2,1)S(1)}, bf16[64,1792]{1,0:T(8,128)(2,1)S(1)}, u32[]{:S(2)}, u32[]{:S(2)}) collective-permute-start(bf16[64,1792]{1,0:T(8,128)(2,1)S(1)} %get-tuple-element.31), channel_id=1, source_target_pairs={{0,1},{1,0},{2,3},{3,2},{4,5},{5,4},{6,7},{7,6},{8,9},{9,8},{10,11... | collective-permute-start | bytes 688136 | tf_op jit(solution)/shard_map/ppermute | solution.py:421
  24.4 35.4 %collective-permute-start.10 = (bf16[304,896]{1,0:T(8,128)(2,1)}, bf16[304,896]{1,0:T(8,128)(2,1)}, u32[]{:S(2)}, u32[]{:S(2)}) collective-permute-start(bf16[304,896]{1,0:T(8,128)(2,1)} %collective-permute-done.9.rest_0_), channel_id=1, source_target_pairs={{0,4},{4,0},{8,12},{12,8},{1,5},{5,1},{9,13},{13,9},{2,6},{6,2},{1... | collective-permute-start | bytes 1634312 | tf_op jit(solution)/shard_map/ppermute | solution.py:391
  28.4 16.3 %collective-permute-start.11 = (bf16[304,896]{1,0:T(8,128)(2,1)}, bf16[304,896]{1,0:T(8,128)(2,1)}, u32[]{:S(2)}, u32[]{:S(2)}) collective-permute-start(bf16[304,896]{1,0:T(8,128)(2,1)} %collective-permute-done.9.rest_0_), channel_id=1, source_target_pairs={{0,16},{16,0},{1,17},{17,1},{2,18},{18,2},{3,19},{19,3},{4,20},{20... | collective-permute-start | bytes 1634312 | tf_op jit(solution)/shard_map/ppermute | solution.py:426
  31.1 30.3 %collective-permute-start.14 = (bf16[64,1792]{1,0:T(8,128)(2,1)}, bf16[64,1792]{1,0:T(8,128)(2,1)}, u32[]{:S(2)}, u32[]{:S(2)}) collective-permute-start(bf16[64,1792]{1,0:T(8,128)(2,1)} %add_convert_fusion.1.rest_1_), channel_id=1, source_target_pairs={{0,2},{1,3},{2,0},{3,1},{4,6},{5,7},{6,4},{7,5},{8,10},{9,11},{10,... | collective-permute-start | bytes 688136 | tf_op jit(solution)/shard_map/ppermute | solution.py:423
  40.5 20.9 %collective-permute-start.13 = (bf16[64,1792]{1,0:T(8,128)(2,1)}, bf16[64,1792]{1,0:T(8,128)(2,1)}, u32[]{:S(2)}, u32[]{:S(2)}) collective-permute-start(bf16[64,1792]{1,0:T(8,128)(2,1)} %add_convert_fusion.2.rest_0_), channel_id=1, source_target_pairs={{0,2},{1,3},{2,0},{3,1},{4,6},{5,7},{6,4},{7,5},{8,10},{9,11},{10,... | collective-permute-start | bytes 688136 | tf_op jit(solution)/shard_map/ppermute | solution.py:423
  44.7 15.1 %collective-permute-start.12 = (bf16[304,896]{1,0:T(8,128)(2,1)}, bf16[304,896]{1,0:T(8,128)(2,1)}, u32[]{:S(2)}, u32[]{:S(2)}) collective-permute-start(bf16[304,896]{1,0:T(8,128)(2,1)} %collective-permute-done.11.rest_2_), channel_id=1, source_target_pairs={{0,4},{4,0},{8,12},{12,8},{1,5},{5,1},{9,13},{13,9},{2,6},{6,2},{1... | collective-permute-start | bytes 1634312 | tf_op jit(solution)/shard_map/ppermute | solution.py:391
  49.0 10.8 %collective-permute-start.8 = (bf16[64,304]{1,0:T(8,128)(2,1)S(1)}, bf16[64,304]{1,0:T(8,128)(2,1)S(1)}, u32[]{:S(2)}, u32[]{:S(2)}) collective-permute-start(bf16[64,304]{1,0:T(8,128)(2,1)S(1)} %get-tuple-element.34), channel_id=1, source_target_pairs={{0,1},{1,0},{2,3},{3,2},{4,5},{5,4},{6,7},{7,6},{8,9},{9,8},{10,11... | collective-permute-start | bytes 116744 | tf_op jit(solution)/shard_map/ppermute | solution.py:429

commit v2 on v1

v2 whole, which is shorter than its diff:
```python
import functools

import jax
import jax.numpy as jnp
from jax import lax
from jax.experimental import pallas as pl
from jax.experimental.pallas import tpu as pltpu
from jax.sharding import PartitionSpec as P

KV_HEADS = 4
HEAD_DIM = 128
BLOCK = 128
LANES = 128
MASKED = -1e30
EXP2_SCALE = 1.4426950408889634 / (HEAD_DIM**0.5)
BF16 = jnp.bfloat16
F32 = jnp.float32
OVER_LAST = (((1,), (1,)), ((), ()))
WIDE = 256


def fill_bias(bias_ref, mask_ref, labels_ref, here, shards):
    key_in = lax.broadcasted_iota(jnp.int32, (BLOCK, BLOCK), 0)
    query_in = lax.broadcasted_iota(jnp.int32, (BLOCK, BLOCK), 1)
    later = (key_in > query_in).astype(jnp.int32)
    piece_blocks = bias_ref.shape[1] // BLOCK
    any_open = jnp.int32(0)
    for c, shard_of in enumerate(shards):
        for b in range(piece_blocks):
            other = shard_of * piece_blocks + b
            is_open = mask_ref[0, here, other]
            any_open = any_open | is_open
            closed = jnp.where(other == here, 1 - labels_ref[0, here], 0) * later
            closed = jnp.where(is_open == 1, closed, 1)
            bias_ref[c, b * BLOCK : (b + 1) * BLOCK, :] = jnp.where(closed == 1, MASKED, 0.0).astype(BF16)
    return any_open


def attend(q_ref, key_refs, value_refs, bias_ref, s_buf, prior, finish):
    tile, width = q_ref.shape
    group = width // (KV_HEADS * HEAD_DIM)
    rows = group * tile
    row_ids = lax.broadcasted_iota(jnp.int32, (tile, BLOCK), 0)
    col_ids = lax.broadcasted_iota(jnp.int32, (tile, BLOCK), 1)
    picks = jnp.where(row_ids == col_ids, 1.0, 0.0).astype(BF16)
    ones = jnp.ones((key_refs[0].shape[0], HEAD_DIM), BF16)
    limits = {}

    def score(g):
        q_all = jnp.concatenate(
            [
                jnp.concatenate([q_ref[:, (g * group + h) * HEAD_DIM : (g * group + h + 1) * HEAD_DIM], picks], axis=1)
                for h in range(group)
            ],
            axis=0,
        )
        lanes = slice(g * HEAD_DIM, (g + 1) * HEAD_DIM)
        k_all = jnp.concatenate(
            [jnp.concatenate([ref[:, lanes], bias_ref[c]], axis=1) for c, ref in enumerate(key_refs)], axis=0
        )
        s = lax.dot_general(q_all, k_all, OVER_LAST, preferred_element_type=F32)
        s_buf[g % 2] = s
        top = functools.reduce(jnp.maximum, [s[:, n : n + LANES] for n in range(0, s.shape[1], LANES)])
        top = jnp.broadcast_to(jnp.max(top, axis=1, keepdims=True), (rows, LANES))
        if prior is not None:
            top = jnp.maximum(top, prior(g)[2])
        limits[g] = top

    def mix(g):
        lanes = slice(g * HEAD_DIM, (g + 1) * HEAD_DIM)
        shift = limits[g] * EXP2_SCALE
        soft = jnp.concatenate(
            [
                jnp.exp2(s_buf[g % 2, :, n : n + LANES] * EXP2_SCALE - shift).astype(BF16)
                for n in range(0, s_buf.shape[2], LANES)
            ],
            axis=1,
        )
        v_all = jnp.concatenate([jnp.concatenate([ref[:, lanes], ones], axis=1) for ref in value_refs], axis=0)
        mixed = jnp.dot(soft, v_all, preferred_element_type=F32)
        sums, totals = mixed[:, :HEAD_DIM], mixed[:, HEAD_DIM:]
        if prior is not None:
            before = prior(g)
            factor = jnp.exp2((before[2] - limits[g]) * EXP2_SCALE)
            sums = sums + before[0] * factor
            totals = totals + before[1] * factor
        finish(g, sums, totals, limits[g])

    score(0)
    for g in range(KV_HEADS):
        if g + 1 < KV_HEADS:
            score(g + 1)
        mix(g)


def quarters_kernel(place_ref, wd_hbm, *rest):
    out_refs, sem = rest[:-1], rest[-1]
    low, core = place_ref[2], place_ref[3]
    width = wd_hbm.shape[1]
    copies = []
    for i, half in enumerate((1 - low, low)):
        cols = pl.ds(pl.multiple_of(half * (width // 2) + core * (width // 4), LANES), width // 4)
        copies.append(pltpu.make_async_copy(wd_hbm.at[:, cols], out_refs[i], sem.at[i]))
    for copy in copies:
        copy.start()
    for copy in copies:
        copy.wait()


def near_kernel(split, labels_ref, mask_ref, place_ref, q_hbm, k_hbm, v_hbm, k_ref, v_ref, *rest):
    k_buf, v_buf, bias_buf, s_buf, sem, kv_sem = rest[-6:]
    blocks = len(rest[:-6]) // 4
    outs = [rest[4 * i : 4 * i + 4] for i in range(blocks)]
    tile = outs[0][3].shape[0]
    ctx_here, section = place_ref[0], place_ref[1]
    order = [1 - section, section] if split else list(range(blocks))

    loads = [
        pltpu.make_async_copy(q_hbm.at[pl.ds(pl.multiple_of(t * tile, tile), tile)], outs[i][3], sem.at[i])
        for i, t in enumerate(order)
    ]
    loads.append(pltpu.make_async_copy(k_hbm, k_buf, kv_sem.at[0]))
    loads.append(pltpu.make_async_copy(v_hbm, v_buf, kv_sem.at[1]))
    for copy in loads:
        copy.start()
    for i, t in enumerate(order):
        fill_bias(bias_buf.at[i], mask_ref, labels_ref, ctx_here * blocks + t, [ctx_here, ctx_here ^ 1])
    for copy in loads:
        copy.wait()

    for i, t in enumerate(order):
        sums_ref, totals_ref, limits_ref, q_ref = outs[i]

        @pl.when(labels_ref[0, ctx_here * blocks + t] == section)
        def _():
            def finish(g, sums, totals, limit):
                sums_ref[g] = sums
                totals_ref[g] = totals
                limits_ref[g] = limit

            attend(q_ref, [k_buf, k_ref], [v_buf, v_ref], bias_buf.at[i], s_buf, None, finish)


def attend_far(match, here, pieces, refs, att_ref, bias_buf, s_buf):
    labels_ref, mask_ref, place_ref, key_refs, value_refs, sums_ref, totals_ref, limits_ref, q_ref = refs
    tile, width = att_ref.shape
    group = width // (KV_HEADS * HEAD_DIM)
    opened = fill_bias(bias_buf, mask_ref, labels_ref, here, [place_ref[0] ^ c for c in pieces])

    def finish(g, sums, totals, _):
        attended = (sums / totals).astype(BF16)
        for h in range(group):
            at = (g * group + h) * HEAD_DIM
            att_ref[:, at : at + HEAD_DIM] = attended[h * tile : (h + 1) * tile]

    def prior(g):
        return sums_ref[g], totals_ref[g], limits_ref[g]

    @pl.when(match & (opened > 0))
    def _():
        attend(q_ref, key_refs, value_refs, bias_buf, s_buf, prior, finish)

    @pl.when(match & (opened == 0))
    def _():
        for g in range(KV_HEADS):
            finish(g, sums_ref[g], totals_ref[g], None)


def norm_block(gains_ref, section, first_row, tile, mid_of, norm_buf):
    gain = gains_ref[pl.ds(section, 1), :]
    step = 16

    def norm_rows(j, carry):
        rows = pl.ds(pl.multiple_of(first_row + j * step, step), step)
        mid = mid_of(rows, slice(None))
        factor = lax.rsqrt(jnp.mean(mid * mid, axis=-1, keepdims=True) + 1e-05)
        norm_buf[rows, :] = (mid * factor * gain).astype(BF16)
        return carry

    lax.fori_loop(0, tile // step, norm_rows, 0)


def hidden_of(norm_buf, w_ref, units):
    up_at = w_ref.shape[0] - units
    both = lax.dot_general(norm_buf[...], w_ref[...], OVER_LAST, preferred_element_type=F32)
    gate, upper = both[:, :units], both[:, up_at : up_at + units]
    return (gate * upper / (1.0 + jnp.exp(-gate))).astype(BF16)


def halves_of(place_ref, tile):
    half = tile // 2
    low = place_ref[2]
    own = pl.ds(pl.multiple_of(low * half, half), half)
    return own, pl.ds(pl.multiple_of(half - low * half, half), half)


def far_kernel(split, pieces, labels_ref, mask_ref, place_ref, res_hbm, gains_ref, *rest):
    tile, width = rest[3].shape
    blocks = res_hbm.shape[0] // tile
    state_refs, rest = rest[: 4 * blocks], rest[4 * blocks :]
    count = len(pieces)
    key_refs, value_refs = rest[:count], rest[count : 2 * count]
    wg_hbm, wu_hbm, wd_hbm = rest[2 * count : 2 * count + 3]
    out_refs = rest[2 * count + 3 : -10]
    res_buf, w_buf, wd_buf, bias_buf, s_buf, att_buf, norm_buf, hid_buf, sem, w_sem = rest[-10:]
    units = wg_hbm.shape[0]
    ctx_here, section, first = place_ref[0], place_ref[1], place_ref[4]
    chosen = [1 - section, section] if split else list(range(blocks))
    refs = (labels_ref, mask_ref, place_ref, key_refs, value_refs)

    loads = []
    for i, t in enumerate(chosen):
        rows = pl.ds(pl.multiple_of(t * tile, tile), tile)
        loads.append(pltpu.make_async_copy(res_hbm.at[rows], res_buf.at[pl.ds(i * tile, tile)], sem.at[i]))
    loads.append(pltpu.make_async_copy(wg_hbm, w_buf.at[pl.ds(0, units)], w_sem.at[0]))
    loads.append(pltpu.make_async_copy(wu_hbm, w_buf.at[pl.ds(w_buf.shape[0] - units, units)], w_sem.at[1]))
    later = pltpu.make_async_copy(wd_hbm, wd_buf, w_sem.at[2])
    for copy in loads:
        copy.start()
    later.start()

    matches = [labels_ref[0, ctx_here * blocks + t] == section for t in chosen]
    for i, t in enumerate(chosen):
        span = pl.ds(i * tile, tile)
        block_refs = (*refs, *state_refs[4 * i : 4 * i + 4])
        attend_far(matches[i], ctx_here * blocks + t, pieces, block_refs, att_buf.at[span], bias_buf, s_buf)

        @pl.when(jnp.logical_not(matches[i]))
        def _():
            norm_buf[span, :] = jnp.zeros((tile, width), BF16)

    for copy in loads:
        copy.wait()

    def mid_of(rows, cols):
        return res_buf[rows, cols].astype(F32) + att_buf[rows, cols].astype(F32)

    for i in range(len(chosen)):

        @pl.when(matches[i])
        def _():
            norm_block(gains_ref, section, i * tile, tile, mid_of, norm_buf)

    later.wait()

    @pl.when(functools.reduce(jnp.logical_or, matches))
    def _():
        hid_buf[...] = hidden_of(norm_buf, w_buf, units)
        if split:
            send_ref, keep_ref, terms_ref, mid_ref = out_refs
            own, other = [pl.ds(pl.multiple_of(span.start + tile, span.size), span.size) for span in halves_of(place_ref, tile)]
            send_ref[:tile, :] = hid_buf[:tile, :]
            send_ref[tile:, :] = hid_buf[other, :]
            keep_ref[...] = hid_buf[own, :]
            for n in range(0, width // 2, WIDE):
                cols = pl.ds(pl.multiple_of(place_ref[2] * (width // 2) + n, LANES), WIDE)
                terms = jnp.dot(hid_buf[:tile, :], wd_buf[:, cols], preferred_element_type=F32)
                terms_ref[:, n : n + WIDE] = terms + mid_of(slice(0, tile), cols)
            for n in range(0, width, WIDE):
                mid_ref[:, n : n + WIDE] = mid_of(own, slice(n, n + WIDE))
        else:
            for n in range(0, width, WIDE):
                cols = slice(n, n + WIDE)
                terms = jnp.dot(hid_buf[...], wd_buf[:, cols], preferred_element_type=F32)
                for i in range(blocks):
                    span = slice(i * tile, (i + 1) * tile)
                    kept = terms[span] + mid_of(span, cols) * first.astype(F32)
                    out_refs[0][span, cols] = jnp.where(matches[i], kept, 0.0)

    if not split:

        @pl.when(jnp.logical_not(functools.reduce(jnp.logical_or, matches)))
        def _():
            out_refs[0][...] = jnp.zeros(out_refs[0].shape, F32)


def down_leave_kernel(labels_ref, place_ref, in_ref, base_ref, here_ref, there_ref, after_ref, same_ref, other_ref, token_ref):
    tile, quarter = base_ref.shape[0], here_ref.shape[1]
    ctx_here, section, core = place_ref[0], place_ref[1], place_ref[3]
    match = labels_ref[0, ctx_here * 2 + 1 - section] == section
    token_ref[...] = jnp.zeros(token_ref.shape, F32)
    rows = halves_of(place_ref, tile)

    @pl.when(match)
    def _():
        left = jnp.concatenate([in_ref[span, :] for span in rows], axis=0)
        for from_core, ref in ((core, here_ref), (1 - core, there_ref)):
            for n in range(0, quarter, WIDE):
                wide = min(WIDE, quarter - n)
                cols = pl.ds(pl.multiple_of(from_core * quarter + n, LANES), wide)
                terms = jnp.dot(left, ref[:, n : n + wide], preferred_element_type=F32)
                for i, to_ref in enumerate((same_ref, other_ref)):
                    part = terms[i * tile // 2 : (i + 1) * tile // 2] + base_ref[rows[i], cols]
                    to_ref[:, cols] = part.astype(BF16)

    @pl.when(jnp.logical_not(match))
    def _():
        same_ref[...] = jnp.zeros(same_ref.shape, BF16)
        other_ref[...] = jnp.zeros(other_ref.shape, BF16)


def down_stay_kernel(labels_ref, place_ref, in_ref, keep_ref, mid_ref, after_ref, wd_hbm, *rest):
    quarter_refs, (out_ref, wd_buf, sem) = rest[:-3], rest[-3:]
    quarter = quarter_refs[0].shape[1]
    rows = keep_ref.shape[0]
    ctx_here, section, low, core = place_ref[0], place_ref[1], place_ref[2], place_ref[3]
    match = labels_ref[0, ctx_here * 2 + section] == section

    @pl.when(match)
    def _():
        copy = pltpu.make_async_copy(wd_hbm, wd_buf, sem)
        copy.start()
        copy.wait()
        arrived = in_ref[in_ref.shape[0] - rows :, :]
        for i, ref in enumerate(quarter_refs):
            half = low if i < 2 else 1 - low
            from_core = core if i % 2 == 0 else 1 - core
            for n in range(0, quarter, WIDE):
                wide = min(WIDE, quarter - n)
                cols = pl.ds(pl.multiple_of((2 * half + from_core) * quarter + n, LANES), wide)
                terms = jnp.dot(arrived, ref[:, n : n + wide], preferred_element_type=F32)
                terms = terms + jnp.dot(keep_ref[...], wd_buf[:, cols], preferred_element_type=F32)
                out_ref[:, cols] = terms + mid_ref[:, cols]

    @pl.when(jnp.logical_not(match))
    def _():
        out_ref[...] = jnp.zeros(out_ref.shape, F32)


def last_sum_kernel(place_ref, staying_ref, same_ref, other_ref, out_ref):
    half = same_ref.shape[1]
    low = place_ref[2]
    for at, ref in ((low, same_ref), (1 - low, other_ref)):
        for n in range(0, half, WIDE):
            cols = pl.ds(pl.multiple_of(at * half + n, LANES), WIDE)
            out_ref[:, cols] = (staying_ref[:, cols] + ref[:, n : n + WIDE].astype(F32)).astype(BF16)


SMEM = pl.BlockSpec(memory_space=pltpu.SMEM)
HBM = pl.BlockSpec(memory_space=pltpu.HBM)
VMEM = pl.BlockSpec(memory_space=pltpu.VMEM)
ANY = pl.BlockSpec(memory_space=pl.ANY)


def params(mib):
    return pltpu.CompilerParams(vmem_limit_bytes=mib * 1024 * 1024)


def stay(array):
    return pltpu.with_memory_space_constraint(array, pltpu.HBM)


def cost(flops, moved, powers=0):
    return pl.CostEstimate(flops=flops, bytes_accessed=moved, transcendentals=powers)


def w_down_quarters(place, wd):
    units, width = wd.shape
    return pl.pallas_call(
        quarters_kernel,
        out_shape=[jax.ShapeDtypeStruct((units, width // 4), BF16)] * 2,
        in_specs=[SMEM, HBM],
        out_specs=[VMEM] * 2,
        scratch_shapes=[pltpu.SemaphoreType.DMA((2,))],
        compiler_params=params(8),
        cost_estimate=cost(units, units * width),
    )(place, wd)


def near_attention(split, labels, mask, place, queries, own_key, own_value, key, value):
    shard, width = queries.shape
    blocks = shard // BLOCK
    piece_rows, kv_width = key.shape
    rows = width // (KV_HEADS * HEAD_DIM) * BLOCK
    count = 2 * piece_rows
    shape = jax.ShapeDtypeStruct
    state = shape((KV_HEADS, rows, LANES), F32)
    outs = [state, state, state, shape((BLOCK, width), BF16)] * blocks
    made = pl.pallas_call(
        functools.partial(near_kernel, split),
        out_shape=outs,
        in_specs=[SMEM, SMEM, SMEM, HBM, HBM, HBM, VMEM, VMEM],
        out_specs=[VMEM] * len(outs),
        scratch_shapes=[
            pltpu.VMEM((piece_rows, kv_width), BF16),
            pltpu.VMEM((piece_rows, kv_width), BF16),
            pltpu.VMEM((blocks, 2, piece_rows, BLOCK), BF16),
            pltpu.VMEM((2, rows, count), F32),
            pltpu.SemaphoreType.DMA((blocks,)),
            pltpu.SemaphoreType.DMA((2,)),
        ],
        compiler_params=params(16),
        cost_estimate=cost(800 * shard * width * count, 2 * shard * width, shard * width // HEAD_DIM * count),
    )(labels, mask, place, queries, own_key, own_value, key, value)
    return [list(made[4 * i : 4 * i + 4]) for i in range(blocks)]


def far_attention(split, pieces, labels, mask, place, residual, gains, states, keys, values, wg, wu, wd):
    tile, width = states[0][3].shape
    piece_rows = keys[0].shape[0]
    rows = width // (KV_HEADS * HEAD_DIM) * BLOCK
    count = piece_rows * len(pieces)
    units = wg.shape[0]
    up_at = -(-units // LANES) * LANES
    taken = tile * len(states)
    shape = jax.ShapeDtypeStruct
    if split:
        outs = [shape((tile + tile // 2, units), BF16), shape((tile // 2, units), BF16)]
        outs += [shape((tile, width // 2), F32), shape((tile // 2, width), F32)]
    else:
        outs = [shape((taken, width), F32)]
    return pl.pallas_call(
        functools.partial(far_kernel, split, pieces),
        out_shape=outs,
        in_specs=[SMEM, SMEM, SMEM, HBM, VMEM] + [VMEM] * (4 * len(states) + 2 * len(pieces)) + [HBM] * 3,
        out_specs=[VMEM] * len(outs),
        scratch_shapes=[
            pltpu.VMEM((taken, width), BF16),
            pltpu.VMEM((up_at + units, width), BF16),
            pltpu.VMEM(wd.shape, BF16),
            pltpu.VMEM((len(pieces), piece_rows, BLOCK), BF16),
            pltpu.VMEM((2, rows, count), F32),
            pltpu.VMEM((taken, width), BF16),
            pltpu.VMEM((taken, width), BF16),
            pltpu.VMEM((taken, units), BF16),
            pltpu.SemaphoreType.DMA((len(states),)),
            pltpu.SemaphoreType.DMA((3,)),
        ],
        compiler_params=params(28),
        cost_estimate=cost(taken * width, width, taken),
    )(
        labels, mask, place, residual, gains, *[array for state in states for array in state],
        *keys, *values, wg, wu, wd,
    )


TOKEN = jax.ShapeDtypeStruct((8, LANES), F32)


def down_leave(labels, place, arrived, base, here, there, after):
    tile, half_width = base.shape
    half = jax.ShapeDtypeStruct((tile // 2, half_width), BF16)
    return pl.pallas_call(
        down_leave_kernel,
        out_shape=[half, half, TOKEN],
        in_specs=[SMEM, SMEM] + [VMEM] * 4 + [ANY],
        out_specs=[VMEM] * 3,
        compiler_params=params(16),
        cost_estimate=cost(tile, tile),
    )(labels, place, arrived, base, here, there, after)


def down_stay(labels, place, arrived, keep, mid, after, wd, *quarters):
    rows, units = keep.shape
    return pl.pallas_call(
        down_stay_kernel,
        out_shape=jax.ShapeDtypeStruct(mid.shape, F32),
        in_specs=[SMEM, SMEM, VMEM, VMEM, VMEM, ANY, HBM] + [VMEM] * len(quarters),
        out_specs=VMEM,
        scratch_shapes=[pltpu.VMEM(wd.shape, BF16), pltpu.SemaphoreType.DMA(())],
        compiler_params=params(16),
        cost_estimate=cost(8000 * rows * wd.size, wd.size),
    )(labels, place, arrived, keep, mid, after, wd, *quarters)


def last_sum(place, staying, same, other):
    return pl.pallas_call(
        last_sum_kernel,
        out_shape=jax.ShapeDtypeStruct(staying.shape, BF16),
        in_specs=[SMEM] + [VMEM] * 3,
        out_specs=VMEM,
        compiler_params=params(8),
        cost_estimate=cost(staying.size, staying.size),
    )(place, staying, same, other)


def xor_pairs(count, bits):
    return [(i, i ^ bits) for i in range(count)]


def per_device(queries, keys, values, residual, labels, block_mask, gains, w_gate, w_up, w_down):
    shard, width = queries.shape[1:]
    exp_count = lax.axis_size("exp")
    exp_here = lax.axis_index("exp")
    ctx_count = lax.axis_size("ctx")
    ctx_here = lax.axis_index("ctx")
    half = exp_count // 2
    split = exp_count == 4 and shard == 2 * BLOCK and ctx_count == 4
    section = exp_here // half
    low = exp_here % 2 if split else jnp.zeros_like(exp_here)
    core = ctx_here % 2
    first = exp_here % half == 0
    place = jnp.stack([value.astype(jnp.int32) for value in (ctx_here, section, low, core, first)])
    labels, block_mask, gains = stay(labels), stay(block_mask), stay(gains)
    own_q, own_res = stay(queries[0]), stay(residual[0])

    held = {0: (keys[0], values[0])}

    def spread(bits):
        pairs = xor_pairs(ctx_count, bits)
        for at, (k, v) in list(held.items()):
            held[at ^ bits] = (lax.ppermute(k, "ctx", pairs), lax.ppermute(v, "ctx", pairs))

    def swap(array):
        return lax.ppermute(array, "ctx", xor_pairs(ctx_count, 1))

    bits = ctx_count // 2
    while bits > 1:
        spread(bits)
        bits //= 2
    held[1] = (swap(keys[0]), swap(values[0]))
    z_pairs = xor_pairs(exp_count, 1)
    if split:
        here, late = w_down_quarters(place, stay(w_down))
        late, key = lax.optimization_barrier((late, held[1][0]))
        held[1] = (key, held[1][1])
        here, late = lax.ppermute(here, "exp", z_pairs), lax.ppermute(late, "exp", z_pairs)
    states = near_attention(
        split, labels, block_mask, place, own_q, stay(keys[0]), stay(values[0]), *held[1]
    )
    for at in range(2, ctx_count, 2):
        k, v = held[at]
        k, v, states[0][0] = lax.optimization_barrier((k, v, states[0][0]))
        held[at] = (k, v)
        held[at + 1] = (swap(k), swap(v))
    far = range(2, ctx_count)
    far_keys, far_values = [held[c][0] for c in far], [held[c][1] for c in far]
    weights = (far_keys, far_values, stay(w_gate.T), stay(w_up.T), stay(w_down))
    shared = (labels, block_mask, place, own_res, gains)
    made = far_attention(split, far, *shared, states, *weights)
    if not split:
        return lax.psum_scatter(made[0][None], "exp", scatter_dimension=1, tiled=True).astype(BF16)

    send, keep, base, mid = made
    here, send = lax.optimization_barrier((here, send))
    there = swap(here)
    arrived = lax.ppermute(send, "exp", z_pairs)
    same, other, token = down_leave(labels, place, arrived, base, here, there, late)
    late, token = lax.optimization_barrier((late, token))
    same, other = (
        lax.ppermute(part, "exp", xor_pairs(exp_count, bits)) for part, bits in ((same, 2), (other, 3))
    )
    staying = down_stay(labels, place, arrived, keep, mid, token, stay(w_down), here, there, late, swap(late))
    return last_sum(place, staying, same, other)[None]


def solution(mesh):
    placed = (
        P("dp", "ctx", None),
        P("dp", "ctx", None),
        P("dp", "ctx", None),
        P("dp", "ctx", None),
        P("dp", None),
        P("dp", None, None),
        P(),
        P(None, "exp"),
        P(None, "exp"),
        P("exp", None),
    )
    return jax.shard_map(
        per_device,
        mesh=mesh,
        in_specs=placed,
        out_specs=P("dp", ("ctx", "exp"), None),
        check_vma=False,
    )
```

time: 63.7 us -> 63.7 us (level)
  the two profiles are of different devices: /device:TPU:0 before, /device:TPU:14 now
where the time goes in v2:
time: 63.7 us; the launch traced here: 62.9 us
  waiting for transfers between devices  35.4 us (56%)
  Pallas kernels  14.5 us (23%)
  starting transfers between devices  12.9 us (20%)
    ppermute x2, waiting for transfers between devices, per_device(): lax.ppermute(part, 'exp', xor_pairs(exp_count, bits))  19.3 us
    ppermute x1, waiting for transfers between devices, per_device(): arrived = lax.ppermute(send, 'exp', z_pairs)  8.38 us
    ppermute x6, starting transfers between devices, swap(): return lax.ppermute(array, 'ctx', xor_pairs(ctx_count, 1))  4.89 us
    ppermute x1, waiting for transfers between devices, spread(): lax.ppermute(v, 'ctx', pairs)  4.66 us
    pallas_call x1, Pallas kernels, far_attention(): pl.pallas_call(functools.partial(far_kernel, split, pieces), out_shape=ou...  4.56 us
    ppermute x2, starting transfers between devices, per_device(): lax.ppermute(part, 'exp', xor_pairs(exp_count, bits))  4.53 us
    pallas_call x1, Pallas kernels, w_down_quarters(): pl.pallas_call(quarters_kernel, out_shape=[jax.ShapeDtypeStruct((units, w...  2.61 us
    pallas_call x1, Pallas kernels, near_attention(): pl.pallas_call(functools.partial(near_kernel, split), out_shape=outs, in_...  2.36 us
  transfers between devices with their start and end apart: 13, of which 7 were waited for; matrix products, arithmetic and copies ran while one was open for 0% of the time, Pallas kernels for 17%

profile of v2, /device:TPU:14, one launch (start us, length us, event | category | flops | bytes accessed | tf_op | source)
XLA Modules:
  0.0 62.9 jit_solution(583536292850735741)
XLA Ops:
  0.0 0.0 collective-permute-start.3
  0.0 0.5 collective-permute-start.4
  0.5 0.5 collective-permute-start.1
  1.0 1.5 %collective-permute-start.2 = (bf16[256,512]{1,0:T(8,128)(2,1)}, bf16[256,512]{1,0:T(8,128)(2,1)}, u32[]{:S(2)}, u32[]{:S(2)}) collective-permute-start(bf16[256,512]{1,0:T(8,128)(2,1)} %bitcast.20), channel_id=1, source_target_pairs={{0,8},{4,12},{8,0},{12,4},{1,9},{5,13},{9,1},{13,5},{2,10},{6,14},... | collective-permute-start | bytes 786440 | tf_op jit(solution)/shard_map/ppermute | solution.py:502
  2.5 0.1 stack.27.place_ref
  2.6 2.6 %shard_map.100 = (bf16[304,896]{1,0:T(8,128)(2,1)}, bf16[304,896]{1,0:T(8,128)(2,1)S(1)}) custom-call(s32[5]{0:T(128)S(1)} %stack.27.place_ref, bf16[304,3584]{1,0:T(8,128)(2,1)} %wd_hbm.3), custom_call_target="tpu_custom_call" | custom-call | flops 304 | bytes 1089536 | tf_op jit(solution)/shard_map/pallas_call | solution.py:359
  5.2 0.5 collective-permute-start
  5.8 0.0 collective-permute-done.3.k_ref
  5.8 0.0 collective-permute-done.4.v_ref
  5.8 2.4 %shard_map.101 = (f32[4,896,128]{2,1,0:T(8,128)S(1)}, f32[4,896,128]{2,1,0:T(8,128)S(1)}, f32[4,896,128]{2,1,0:T(8,128)S(1)}, bf16[128,3584]{1,0:T(8,128)(2,1)S(...) custom-call(s32[1,8]{1,0:T(1,128)} %labels_ref.7, ...), custom_call_target="tpu_custom_call" | custom-call | flops 375809638400 | bytes 1835008 | tf_op jit(solution)/shard_map/pallas_call | solution.py:379
  8.1 1.9 %collective-permute-done.1.rest_8_ = bf16[256,512]{1,0:T(8,128)(2,1)} collective-permute-done((bf16[256,512]{1,0:T(8,128)(2,1)}, bf16[256,512]{1,0:T(8,128)(2,1)}, u32[]{:S(2)}, u32[]{:S(2)}) %collective-permute-start.1) | collective-permute-done | bytes 262176 | tf_op jit(solution)/shard_map/ppermute | solution.py:502
  10.0 4.7 %collective-permute-done.2.rest_10_ = bf16[256,512]{1,0:T(8,128)(2,1)} collective-permute-done((bf16[256,512]{1,0:T(8,128)(2,1)}, bf16[256,512]{1,0:T(8,128)(2,1)}, u32[]{:S(2)}, u32[]{:S(2)}) %collective-permute-start.2) | collective-permute-done | bytes 262176 | tf_op jit(solution)/shard_map/ppermute | solution.py:502
  14.7 0.0 collective-permute-start.5
  14.7 0.5 collective-permute-start.6
  15.2 0.4 collective-permute-start.8
  15.6 0.8 %collective-permute-done.5.rest_9_ = bf16[256,512]{1,0:T(8,128)(2,1)S(1)} collective-permute-done((bf16[256,512]{1,0:T(8,128)(2,1)}, bf16[256,512]{1,0:T(8,128)(2,1)S(1)}, u32[]{:S(2)}, u32[]{:S(2)}) %collective-permute-start.5) | collective-permute-done | bytes 262176 | tf_op jit(solution)/shard_map/ppermute | solution.py:505
  16.4 0.4 collective-permute-done.6.rest_11_
  16.8 4.6 %shard_map.102 = (bf16[192,304]{1,0:T(8,128)(2,1)S(1)}, bf16[64,304]{1,0:T(8,128)(2,1)S(1)}, f32[128,1792]{1,0:T(8,128)S(1)}, f32[64,3584]{1,0:T(8,128)S(1)}) custom-call(s32[1,8]{1,0:T(1,128)} %labels_ref.7, s32[1,8,8]{2,1,0:T(8,128)} %mask_ref.3, s32[5]{0:T(128)S(1)} %stack.27.place_ref, bf16[256,3584]{1,0:T(8,128)(2,1)} %bitcast.14, f32[2,3584]{1,0:T(2,128)} %gains_ref.1, ...), custom_call_target="tpu_custom_call" | custom-call | flops 917504 | bytes 3584 | tf_op jit(solution)/shard_map/pallas_call | solution.py:412
  21.3 0.0 collective-permute-done.here_ref.rest_0_
  21.4 3.9 %collective-permute-start.9 = (bf16[304,896]{1,0:T(8,128)(2,1)}, bf16[304,896]{1,0:T(8,128)(2,1)S(1)}, u32[]{:S(2)}, u32[]{:S(2)}) collective-permute-start(bf16[304,896]{1,0:T(8,128)(2,1)} %collective-permute-done.here_ref.rest_0_), channel_id=1, source_target_pairs={{0,4},{4,0},{8,12},{12,8},{1,5},{5,1},{9,13},{13,9},{2,6},{6,2},{1... | collective-permute-start | bytes 1634312 | tf_op jit(solution)/shard_map/ppermute | solution.py:505
  25.2 0.5 collective-permute-start.7
  25.7 8.4 %collective-permute-done.7.in_ref = bf16[192,304]{1,0:T(8,128)(2,1)S(1)} collective-permute-done((bf16[192,304]{1,0:T(8,128)(2,1)S(1)}, bf16[192,304]{1,0:T(8,128)(2,1)S(1)}, u32[]{:S(2)}, u32[]{:S(2)}) %collective-permute-start.7) | collective-permute-done | bytes 116768 | tf_op jit(solution)/shard_map/ppermute | solution.py:537
  34.1 0.0 collective-permute-done.8.after_ref.rest_2_
  34.1 0.0 collective-permute-done.9.there_ref.rest_1_
  34.1 1.9 %shard_map.103 = (bf16[64,1792]{1,0:T(8,128)(2,1)}, bf16[64,1792]{1,0:T(8,128)(2,1)}, f32[8,128]{1,0:T(8,128)S(1)}) custom-call(s32[1,8]{1,0:T(1,128)} %labels_ref.7, s32[5]{0:T(128)S(1)} %stack.27.place_ref, bf16[192,304]{1,0:T(8,128)(2,1)S(1)} %collective-permute-done.7.in_ref, f32[128,1792]{1,0:T(8,128)S(1)} %get-tuple-element.50.base_ref, ...), custom_call_target="tpu_custom_call" | custom-call | flops 128 | bytes 128 | tf_op jit(solution)/shard_map/pallas_call | solution.py:443
  35.9 0.0 collective-permute-start.10
  35.9 4.5 %collective-permute-start.11 = (bf16[64,1792]{1,0:T(8,128)(2,1)}, bf16[64,1792]{1,0:T(8,128)(2,1)}, u32[]{:S(2)}, u32[]{:S(2)}) collective-permute-start(bf16[64,1792]{1,0:T(8,128)(2,1)} %get-tuple-element.55), channel_id=1, source_target_pairs={{0,2},{1,3},{2,0},{3,1},{4,6},{5,7},{6,4},{7,5},{8,10},{9,11},{10,... | collective-permute-start | bytes 688136 | tf_op jit(solution)/shard_map/ppermute | solution.py:541
  40.5 0.0 collective-permute-start.12
  40.5 0.0 collective-permute-done.10.rest_3_
  40.5 1.1 %shard_map.104.staying_ref = f32[64,3584]{1,0:T(8,128)S(1)} custom-call(s32[1,8]{1,0:T(1,128)} %labels_ref.7, s32[5]{0:T(128)S(1)} %stack.27.place_ref, bf16[192,304]{1,0:T(8,128)(2,1)S(1)} %collective-permute-done.7.in_ref, bf16[64,304]{1,0:T(8,128)(2,1)S(1)} %get-tuple-element.47.keep_ref, f32[64,3584]{1,0:T(8,128)S(1)} %get-tuple-element.48.mid_ref, ...), custom_call_target="tpu_custom_call" | custom-call | flops 557842432000 | bytes 1089536 | tf_op jit(solution)/shard_map/pallas_call | solution.py:455
  41.6 14.5 %collective-permute-done.11.same_ref = bf16[64,1792]{1,0:T(8,128)(2,1)} collective-permute-done((bf16[64,1792]{1,0:T(8,128)(2,1)}, bf16[64,1792]{1,0:T(8,128)(2,1)}, u32[]{:S(2)}, u32[]{:S(2)}) %collective-permute-start.11) | collective-permute-done | bytes 229408 | tf_op jit(solution)/shard_map/ppermute | solution.py:541
  56.1 4.9 %collective-permute-done.12.other_ref = bf16[64,1792]{1,0:T(8,128)(2,1)} collective-permute-done((bf16[64,1792]{1,0:T(8,128)(2,1)}, bf16[64,1792]{1,0:T(8,128)(2,1)}, u32[]{:S(2)}, u32[]{:S(2)}) %collective-permute-start.12) | collective-permute-done | bytes 229408 | tf_op jit(solution)/shard_map/ppermute | solution.py:541
  61.0 1.9 %shard_map.105 = bf16[64,3584]{1,0:T(8,128)(2,1)} custom-call(s32[5]{0:T(128)S(1)} %stack.27.place_ref, f32[64,3584]{1,0:T(8,128)S(1)} %shard_map.104.staying_ref, bf16[64,1792]{1,0:T(8,128)(2,1)} %collective-permute-done.11.same_ref, bf16[64,1792]{1,0:T(8,128)(2,1)} %collective-permute-done.12.other_ref), custom_call_target="tpu_custom_call" | custom-call | flops 229376 | bytes 229376 | tf_op jit(solution)/shard_map/pallas_call | solution.py:467
Async XLA Ops:
  0.0 5.8 %collective-permute-start.3 = (bf16[256,512]{1,0:T(8,128)(2,1)}, bf16[256,512]{1,0:T(8,128)(2,1)S(1)}, u32[]{:S(2)}, u32[]{:S(2)}) collective-permute-start(bf16[256,512]{1,0:T(8,128)(2,1)} %bitcast.16), channel_id=1, source_target_pairs={{0,4},{4,0},{8,12},{12,8},{1,5},{5,1},{9,13},{13,9},{2,6},{6,2},{1... | collective-permute-start | bytes 786440 | tf_op jit(solution)/shard_map/ppermute | solution.py:505
  0.0 5.8 %collective-permute-start.4 = (bf16[256,512]{1,0:T(8,128)(2,1)}, bf16[256,512]{1,0:T(8,128)(2,1)S(1)}, u32[]{:S(2)}, u32[]{:S(2)}) collective-permute-start(bf16[256,512]{1,0:T(8,128)(2,1)} %bitcast.19), channel_id=1, source_target_pairs={{0,4},{4,0},{8,12},{12,8},{1,5},{5,1},{9,13},{13,9},{2,6},{6,2},{1... | collective-permute-start | bytes 786440 | tf_op jit(solution)/shard_map/ppermute | solution.py:505
  0.5 9.5 %collective-permute-start.1 = (bf16[256,512]{1,0:T(8,128)(2,1)}, bf16[256,512]{1,0:T(8,128)(2,1)}, u32[]{:S(2)}, u32[]{:S(2)}) collective-permute-start(bf16[256,512]{1,0:T(8,128)(2,1)} %bitcast.17), channel_id=1, source_target_pairs={{0,8},{4,12},{8,0},{12,4},{1,9},{5,13},{9,1},{13,5},{2,10},{6,14},... | collective-permute-start | bytes 786440 | tf_op jit(solution)/shard_map/ppermute | solution.py:502
  1.0 13.6 %collective-permute-start.2 = (bf16[256,512]{1,0:T(8,128)(2,1)}, bf16[256,512]{1,0:T(8,128)(2,1)}, u32[]{:S(2)}, u32[]{:S(2)}) collective-permute-start(bf16[256,512]{1,0:T(8,128)(2,1)} %bitcast.20), channel_id=1, source_target_pairs={{0,8},{4,12},{8,0},{12,4},{1,9},{5,13},{9,1},{13,5},{2,10},{6,14},... | collective-permute-start | bytes 786440 | tf_op jit(solution)/shard_map/ppermute | solution.py:502
  5.2 16.1 %collective-permute-start = (bf16[304,896]{1,0:T(8,128)(2,1)}, bf16[304,896]{1,0:T(8,128)(2,1)}, u32[]{:S(2)}, u32[]{:S(2)}) collective-permute-start(bf16[304,896]{1,0:T(8,128)(2,1)} %get-tuple-element.31), channel_id=1, source_target_pairs={{0,1},{1,0},{2,3},{3,2},{4,5},{5,4},{6,7},{7,6},{8,9},{9,8},{10,11... | collective-permute-start | bytes 1634312 | tf_op jit(solution)/shard_map/ppermute | solution.py:517
  14.7 1.7 %collective-permute-start.5 = (bf16[256,512]{1,0:T(8,128)(2,1)}, bf16[256,512]{1,0:T(8,128)(2,1)S(1)}, u32[]{:S(2)}, u32[]{:S(2)}) collective-permute-start(bf16[256,512]{1,0:T(8,128)(2,1)} %collective-permute-done.1.rest_8_), channel_id=1, source_target_pairs={{0,4},{4,0},{8,12},{12,8},{1,5},{5,1},{9,13},{13,9},{2,6},{6,2},{1... | collective-permute-start | bytes 786440 | tf_op jit(solution)/shard_map/ppermute | solution.py:505
  14.7 2.1 %collective-permute-start.6 = (bf16[256,512]{1,0:T(8,128)(2,1)}, bf16[256,512]{1,0:T(8,128)(2,1)S(1)}, u32[]{:S(2)}, u32[]{:S(2)}) collective-permute-start(bf16[256,512]{1,0:T(8,128)(2,1)} %collective-permute-done.2.rest_10_), channel_id=1, source_target_pairs={{0,4},{4,0},{8,12},{12,8},{1,5},{5,1},{9,13},{13,9},{2,6},{6,2},{1... | collective-permute-start | bytes 786440 | tf_op jit(solution)/shard_map/ppermute | solution.py:505
  15.2 18.9 %collective-permute-start.8 = (bf16[304,896]{1,0:T(8,128)(2,1)S(1)}, bf16[304,896]{1,0:T(8,128)(2,1)S(1)}, u32[]{:S(2)}, u32[]{:S(2)}) collective-permute-start(bf16[304,896]{1,0:T(8,128)(2,1)S(1)} %get-tuple-element.49), channel_id=1, source_target_pairs={{0,1},{1,0},{2,3},{3,2},{4,5},{5,4},{6,7},{7,6},{8,9},{9,8},{10,11... | collective-permute-start | bytes 1634312 | tf_op jit(solution)/shard_map/ppermute | solution.py:517
  21.4 12.7 %collective-permute-start.9 = (bf16[304,896]{1,0:T(8,128)(2,1)}, bf16[304,896]{1,0:T(8,128)(2,1)S(1)}, u32[]{:S(2)}, u32[]{:S(2)}) collective-permute-start(bf16[304,896]{1,0:T(8,128)(2,1)} %collective-permute-done.here_ref.rest_0_), channel_id=1, source_target_pairs={{0,4},{4,0},{8,12},{12,8},{1,5},{5,1},{9,13},{13,9},{2,6},{6,2},{1... | collective-permute-start | bytes 1634312 | tf_op jit(solution)/shard_map/ppermute | solution.py:505
  25.2 8.8 %collective-permute-start.7 = (bf16[192,304]{1,0:T(8,128)(2,1)S(1)}, bf16[192,304]{1,0:T(8,128)(2,1)S(1)}, u32[]{:S(2)}, u32[]{:S(2)}) collective-permute-start(bf16[192,304]{1,0:T(8,128)(2,1)S(1)} %get-tuple-element.46), channel_id=1, source_target_pairs={{0,1},{1,0},{2,3},{3,2},{4,5},{5,4},{6,7},{7,6},{8,9},{9,8},{10,11... | collective-permute-start | bytes 350216 | tf_op jit(solution)/shard_map/ppermute | solution.py:537
  35.9 4.5 %collective-permute-start.10 = (bf16[304,896]{1,0:T(8,128)(2,1)S(1)}, bf16[304,896]{1,0:T(8,128)(2,1)S(1)}, u32[]{:S(2)}, u32[]{:S(2)}) collective-permute-start(bf16[304,896]{1,0:T(8,128)(2,1)S(1)} %collective-permute-done.8.after_ref.rest_2_), channel_id=1, source_target_pairs={{0,4},{4,0},{8,12},{12,8},{1,5},{5,1},{9,13},{13,9},{2,6},{6,2},{1... | collective-permute-start | bytes 1634312 | tf_op jit(solution)/shard_map/ppermute | solution.py:505
  35.9 20.1 %collective-permute-start.11 = (bf16[64,1792]{1,0:T(8,128)(2,1)}, bf16[64,1792]{1,0:T(8,128)(2,1)}, u32[]{:S(2)}, u32[]{:S(2)}) collective-permute-start(bf16[64,1792]{1,0:T(8,128)(2,1)} %get-tuple-element.55), channel_id=1, source_target_pairs={{0,2},{1,3},{2,0},{3,1},{4,6},{5,7},{6,4},{7,5},{8,10},{9,11},{10,... | collective-permute-start | bytes 688136 | tf_op jit(solution)/shard_map/ppermute | solution.py:541
  40.5 20.5 %collective-permute-start.12 = (bf16[64,1792]{1,0:T(8,128)(2,1)}, bf16[64,1792]{1,0:T(8,128)(2,1)}, u32[]{:S(2)}, u32[]{:S(2)}) collective-permute-start(bf16[64,1792]{1,0:T(8,128)(2,1)} %get-tuple-element.56), channel_id=1, source_target_pairs={{0,3},{1,2},{2,1},{3,0},{4,7},{5,6},{6,5},{7,4},{8,11},{9,10},{10,... | collective-permute-start | bytes 688136 | tf_op jit(solution)/shard_map/ppermute | solution.py:541

commit v3 on v2

--- a/solution.py
+++ b/solution.py
@@ -93,18 +93,13 @@
         mix(g)
 
 
-def quarters_kernel(place_ref, wd_hbm, *rest):
-    out_refs, sem = rest[:-1], rest[-1]
+def quarter_kernel(place_ref, wd_hbm, out_ref, sem):
     low, core = place_ref[2], place_ref[3]
     width = wd_hbm.shape[1]
-    copies = []
-    for i, half in enumerate((1 - low, low)):
-        cols = pl.ds(pl.multiple_of(half * (width // 2) + core * (width // 4), LANES), width // 4)
-        copies.append(pltpu.make_async_copy(wd_hbm.at[:, cols], out_refs[i], sem.at[i]))
-    for copy in copies:
-        copy.start()
-    for copy in copies:
-        copy.wait()
+    cols = pl.ds(pl.multiple_of((1 - low) * (width // 2) + core * (width // 4), LANES), width // 4)
+    copy = pltpu.make_async_copy(wd_hbm.at[:, cols], out_ref, sem)
+    copy.start()
+    copy.wait()
 
 
 def near_kernel(split, labels_ref, mask_ref, place_ref, q_hbm, k_hbm, v_hbm, k_ref, v_ref, *rest):
@@ -203,6 +198,8 @@
     wg_hbm, wu_hbm, wd_hbm = rest[2 * count : 2 * count + 3]
     out_refs = rest[2 * count + 3 : -10]
     res_buf, w_buf, wd_buf, bias_buf, s_buf, att_buf, norm_buf, hid_buf, sem, w_sem = rest[-10:]
+    if split:
+        send_ref, hid_ref, mid_ref, wd_buf, sent_ref = out_refs
     units = wg_hbm.shape[0]
     ctx_here, section, first = place_ref[0], place_ref[1], place_ref[4]
     chosen = [1 - section, section] if split else list(range(blocks))
@@ -233,7 +230,10 @@
         copy.wait()
 
     def mid_of(rows, cols):
-        return res_buf[rows, cols].astype(F32) + att_buf[rows, cols].astype(F32)
+        mid = res_buf[rows, cols].astype(F32) + att_buf[rows, cols].astype(F32)
+        if split:
+            mid_ref[rows, cols] = mid
+        return mid
 
     for i in range(len(chosen)):
 
@@ -247,17 +247,19 @@
     def _():
         hid_buf[...] = hidden_of(norm_buf, w_buf, units)
         if split:
-            send_ref, keep_ref, terms_ref, mid_ref = out_refs
-            own, other = [pl.ds(pl.multiple_of(span.start + tile, span.size), span.size) for span in halves_of(place_ref, tile)]
+            other = halves_of(place_ref, tile)[1]
+            other = pl.ds(pl.multiple_of(other.start + tile, other.size), other.size)
+            hid_ref[...] = hid_buf[...]
             send_ref[:tile, :] = hid_buf[:tile, :]
             send_ref[tile:, :] = hid_buf[other, :]
-            keep_ref[...] = hid_buf[own, :]
-            for n in range(0, width // 2, WIDE):
-                cols = pl.ds(pl.multiple_of(place_ref[2] * (width // 2) + n, LANES), WIDE)
-                terms = jnp.dot(hid_buf[:tile, :], wd_buf[:, cols], preferred_element_type=F32)
-                terms_ref[:, n : n + WIDE] = terms + mid_of(slice(0, tile), cols)
-            for n in range(0, width, WIDE):
-                mid_ref[:, n : n + WIDE] = mid_of(own, slice(n, n + WIDE))
+
+            @pl.when(matches[1])
+            def _():
+                for n in range(0, width // 2, WIDE):
+                    cols = pl.ds(pl.multiple_of(place_ref[2] * (width // 2) + n, LANES), WIDE)
+                    terms = jnp.dot(hid_buf[other, :], wd_buf[:, cols], preferred_element_type=F32)
+                    sent_ref[:, n : n + WIDE] = terms.astype(BF16)
+
         else:
             for n in range(0, width, WIDE):
                 cols = slice(n, n + WIDE)
@@ -274,7 +276,19 @@
             out_refs[0][...] = jnp.zeros(out_refs[0].shape, F32)
 
 
-def down_leave_kernel(labels_ref, place_ref, in_ref, base_ref, here_ref, there_ref, after_ref, same_ref, other_ref, token_ref):
+def down_own_kernel(labels_ref, place_ref, hid_ref, mid_ref, wd_ref, out_ref):
+    tile, half = out_ref.shape
+    ctx_here, section, low = place_ref[0], place_ref[1], place_ref[2]
+
+    @pl.when(labels_ref[0, ctx_here * 2 + 1 - section] == section)
+    def _():
+        for n in range(0, half, WIDE):
+            cols = pl.ds(pl.multiple_of(low * half + n, LANES), WIDE)
+            terms = jnp.dot(hid_ref[:tile, :], wd_ref[:, cols], preferred_element_type=F32)
+            out_ref[:, n : n + WIDE] = terms + mid_ref[:tile, cols]
+
+
+def down_leave_kernel(labels_ref, place_ref, in_ref, base_ref, here_ref, there_ref, same_ref, other_ref, token_ref):
     tile, quarter = base_ref.shape[0], here_ref.shape[1]
     ctx_here, section, core = place_ref[0], place_ref[1], place_ref[3]
     match = labels_ref[0, ctx_here * 2 + 1 - section] == section
@@ -299,28 +313,29 @@
         other_ref[...] = jnp.zeros(other_ref.shape, BF16)
 
 
-def down_stay_kernel(labels_ref, place_ref, in_ref, keep_ref, mid_ref, after_ref, wd_hbm, *rest):
-    quarter_refs, (out_ref, wd_buf, sem) = rest[:-3], rest[-3:]
-    quarter = quarter_refs[0].shape[1]
-    rows = keep_ref.shape[0]
+def down_stay_kernel(labels_ref, place_ref, in_ref, hid_ref, mid_ref, wd_ref, sum_ref, after_ref, here_ref, there_ref, out_ref):
+    tile, quarter = mid_ref.shape[0] // 2, here_ref.shape[1]
     ctx_here, section, low, core = place_ref[0], place_ref[1], place_ref[2], place_ref[3]
     match = labels_ref[0, ctx_here * 2 + section] == section
+    own = halves_of(place_ref, tile)[0]
+    rows = pl.ds(pl.multiple_of(own.start + tile, own.size), own.size)
 
     @pl.when(match)
     def _():
-        copy = pltpu.make_async_copy(wd_hbm, wd_buf, sem)
-        copy.start()
-        copy.wait()
-        arrived = in_ref[in_ref.shape[0] - rows :, :]
-        for i, ref in enumerate(quarter_refs):
-            half = low if i < 2 else 1 - low
-            from_core = core if i % 2 == 0 else 1 - core
+        arrived = in_ref[tile:, :]
+
+        def base(cols):
+            return jnp.dot(hid_ref[rows, :], wd_ref[:, cols], preferred_element_type=F32) + mid_ref[rows, cols]
+
+        for from_core, ref in ((core, here_ref), (1 - core, there_ref)):
             for n in range(0, quarter, WIDE):
                 wide = min(WIDE, quarter - n)
-                cols = pl.ds(pl.multiple_of((2 * half + from_core) * quarter + n, LANES), wide)
+                cols = pl.ds(pl.multiple_of((2 * low + from_core) * quarter + n, LANES), wide)
                 terms = jnp.dot(arrived, ref[:, n : n + wide], preferred_element_type=F32)
-                terms = terms + jnp.dot(keep_ref[...], wd_buf[:, cols], preferred_element_type=F32)
-                out_ref[:, cols] = terms + mid_ref[:, cols]
+                out_ref[:, cols] = terms + base(cols)
+        for n in range(0, 2 * quarter, WIDE):
+            cols = pl.ds(pl.multiple_of((1 - low) * 2 * quarter + n, LANES), WIDE)
+            out_ref[:, cols] = sum_ref[:, n : n + WIDE].astype(F32) + base(cols)
 
     @pl.when(jnp.logical_not(match))
     def _():
@@ -354,14 +369,14 @@
     return pl.CostEstimate(flops=flops, bytes_accessed=moved, transcendentals=powers)
 
 
-def w_down_quarters(place, wd):
+def w_down_quarter(place, wd):
     units, width = wd.shape
     return pl.pallas_call(
-        quarters_kernel,
-        out_shape=[jax.ShapeDtypeStruct((units, width // 4), BF16)] * 2,
+        quarter_kernel,
+        out_shape=jax.ShapeDtypeStruct((units, width // 4), BF16),
         in_specs=[SMEM, HBM],
-        out_specs=[VMEM] * 2,
-        scratch_shapes=[pltpu.SemaphoreType.DMA((2,))],
+        out_specs=VMEM,
+        scratch_shapes=[pltpu.SemaphoreType.DMA(())],
         compiler_params=params(8),
         cost_estimate=cost(units, units * width),
     )(place, wd)
@@ -390,7 +405,7 @@
             pltpu.SemaphoreType.DMA((2,)),
         ],
         compiler_params=params(16),
-        cost_estimate=cost(800 * shard * width * count, 2 * shard * width, shard * width // HEAD_DIM * count),
+        cost_estimate=cost(40 * shard * width * count, 2 * shard * width, shard * width // HEAD_DIM * count),
     )(labels, mask, place, queries, own_key, own_value, key, value)
     return [list(made[4 * i : 4 * i + 4]) for i in range(blocks)]
 
@@ -405,8 +420,8 @@
     taken = tile * len(states)
     shape = jax.ShapeDtypeStruct
     if split:
-        outs = [shape((tile + tile // 2, units), BF16), shape((tile // 2, units), BF16)]
-        outs += [shape((tile, width // 2), F32), shape((tile // 2, width), F32)]
+        outs = [shape((tile + tile // 2, units), BF16), shape((taken, units), BF16)]
+        outs += [shape((taken, width), F32), shape(wd.shape, BF16), shape((tile // 2, width // 2), BF16)]
     else:
         outs = [shape((taken, width), F32)]
     return pl.pallas_call(
@@ -417,7 +432,7 @@
         scratch_shapes=[
             pltpu.VMEM((taken, width), BF16),
             pltpu.VMEM((up_at + units, width), BF16),
-            pltpu.VMEM(wd.shape, BF16),
+            pltpu.VMEM((16, LANES) if split else wd.shape, BF16),
             pltpu.VMEM((len(pieces), piece_rows, BLOCK), BF16),
             pltpu.VMEM((2, rows, count), F32),
             pltpu.VMEM((taken, width), BF16),
@@ -437,30 +452,41 @@
 TOKEN = jax.ShapeDtypeStruct((8, LANES), F32)
 
 
-def down_leave(labels, place, arrived, base, here, there, after):
+def down_own(labels, place, hid, mid, wd):
+    rows, width = mid.shape
+    return pl.pallas_call(
+        down_own_kernel,
+        out_shape=jax.ShapeDtypeStruct((rows // 2, width // 2), F32),
+        in_specs=[SMEM, SMEM] + [VMEM] * 3,
+        out_specs=VMEM,
+        compiler_params=params(16),
+        cost_estimate=cost(40 * rows * wd.size, wd.size),
+    )(labels, place, hid, mid, wd)
+
+
+def down_leave(labels, place, arrived, base, here, there):
     tile, half_width = base.shape
     half = jax.ShapeDtypeStruct((tile // 2, half_width), BF16)
     return pl.pallas_call(
         down_leave_kernel,
         out_shape=[half, half, TOKEN],
-        in_specs=[SMEM, SMEM] + [VMEM] * 4 + [ANY],
+        in_specs=[SMEM, SMEM] + [VMEM] * 4,
         out_specs=[VMEM] * 3,
         compiler_params=params(16),
         cost_estimate=cost(tile, tile),
-    )(labels, place, arrived, base, here, there, after)
-
-
-def down_stay(labels, place, arrived, keep, mid, after, wd, *quarters):
-    rows, units = keep.shape
+    )(labels, place, arrived, base, here, there)
+
+
+def down_stay(labels, place, arrived, hid, mid, wd, summed, after, here, there):
+    rows, width = mid.shape
     return pl.pallas_call(
         down_stay_kernel,
-        out_shape=jax.ShapeDtypeStruct(mid.shape, F32),
-        in_specs=[SMEM, SMEM, VMEM, VMEM, VMEM, ANY, HBM] + [VMEM] * len(quarters),
+        out_shape=jax.ShapeDtypeStruct((rows // 4, width), F32),
+        in_specs=[SMEM, SMEM] + [VMEM] * 5 + [ANY] + [VMEM] * 2,
         out_specs=VMEM,
-        scratch_shapes=[pltpu.VMEM(wd.shape, BF16), pltpu.SemaphoreType.DMA(())],
         compiler_params=params(16),
-        cost_estimate=cost(8000 * rows * wd.size, wd.size),
-    )(labels, place, arrived, keep, mid, after, wd, *quarters)
+        cost_estimate=cost(40 * rows * wd.size, wd.size),
+    )(labels, place, arrived, hid, mid, wd, summed, after, here, there)
 
 
 def last_sum(place, staying, same, other):
@@ -511,10 +537,7 @@
     held[1] = (swap(keys[0]), swap(values[0]))
     z_pairs = xor_pairs(exp_count, 1)
     if split:
-        here, late = w_down_quarters(place, stay(w_down))
-        late, key = lax.optimization_barrier((late, held[1][0]))
-        held[1] = (key, held[1][1])
-        here, late = lax.ppermute(here, "exp", z_pairs), lax.ppermute(late, "exp", z_pairs)
+        here = lax.ppermute(w_down_quarter(place, stay(w_down)), "exp", z_pairs)
     states = near_attention(
         split, labels, block_mask, place, own_q, stay(keys[0]), stay(values[0]), *held[1]
     )
@@ -531,16 +554,18 @@
     if not split:
         return lax.psum_scatter(made[0][None], "exp", scatter_dimension=1, tiled=True).astype(BF16)
 
-    send, keep, base, mid = made
+    send, hid, mid, own_wd, sent = made
     here, send = lax.optimization_barrier((here, send))
     there = swap(here)
     arrived = lax.ppermute(send, "exp", z_pairs)
-    same, other, token = down_leave(labels, place, arrived, base, here, there, late)
-    late, token = lax.optimization_barrier((late, token))
+    base = down_own(labels, place, hid, mid, own_wd)
+    arrived, sent, base = lax.optimization_barrier((arrived, sent, base))
+    same, other, token = down_leave(labels, place, arrived, base, here, there)
     same, other = (
         lax.ppermute(part, "exp", xor_pairs(exp_count, bits)) for part, bits in ((same, 2), (other, 3))
     )
-    staying = down_stay(labels, place, arrived, keep, mid, token, stay(w_down), here, there, late, swap(late))
+    summed = lax.ppermute(sent, "exp", z_pairs)
+    staying = down_stay(labels, place, arrived, hid, mid, own_wd, summed, token, here, there)
     return last_sum(place, staying, same, other)[None]
 
 

time: 63.7 us -> 58.3 us (0.915); the launches traced: 62.9 us -> 59.4 us
  Pallas kernels: 14.5 us -> 25.8 us
  waiting for transfers between devices: 35.4 us -> 25.8 us
  starting transfers between devices: 12.9 us -> 7.62 us
    pallas_call x1, Pallas kernels: 4.56 us -> 11.7 us  [far_attention(): pl.pallas_call(functools.partial(far_kernel, split, pieces), out_shape=ou...]
    ppermute x2, waiting for transfers between devices: 19.3 us -> 13.8 us  [per_device(): lax.ppermute(part, 'exp', xor_pairs(exp_count, bits))]
    pallas_call x1, Pallas kernels: 2.36 us -> 7.44 us  [near_attention(): pl.pallas_call(functools.partial(near_kernel, split), out_shape=outs, in_...]
    ppermute x1, waiting for transfers between devices: 8.38 us -> 4.36 us  [per_device(): arrived = lax.ppermute(send, 'exp', z_pairs)]
    ppermute x2, waiting for transfers between devices: 0.01 us -> 3.88 us  [the longest x1 3.88 us: per_device(): summed = lax.ppermute(sent, 'exp', z_pairs)]
    ppermute x6 -> x5, starting transfers between devices: 4.89 us -> 1.02 us  [swap(): return lax.ppermute(array, 'ctx', xor_pairs(ctx_count, 1))]
    ppermute x1, waiting for transfers between devices: 4.66 us -> 2.34 us  [spread(): lax.ppermute(v, 'ctx', pairs)]
    ppermute x1, waiting for transfers between devices: 1.87 us -> 0.01 us  [spread(): lax.ppermute(k, 'ctx', pairs)]
  transfers between devices with their start and end apart: 13 -> 12, of which waited for: 7 -> 7; matrix products, arithmetic and copies ran while one was open for 0% -> 0% of each run, Pallas kernels for 17% -> 41%
where the time goes in v3:
time: 58.3 us; the launch traced here: 59.4 us
  Pallas kernels  25.8 us (44%)
  waiting for transfers between devices  25.8 us (44%)
  starting transfers between devices  7.62 us (13%)
    ppermute x2, waiting for transfers between devices, per_device(): lax.ppermute(part, 'exp', xor_pairs(exp_count, bits))  13.8 us
    pallas_call x1, Pallas kernels, far_attention(): pl.pallas_call(functools.partial(far_kernel, split, pieces), out_shape=ou...  11.7 us
    pallas_call x1, Pallas kernels, near_attention(): pl.pallas_call(functools.partial(near_kernel, split), out_shape=outs, in_...  7.44 us
    ppermute x1, waiting for transfers between devices, per_device(): arrived = lax.ppermute(send, 'exp', z_pairs)  4.36 us
    ppermute x1, waiting for transfers between devices, per_device(): summed = lax.ppermute(sent, 'exp', z_pairs)  3.88 us
    ppermute x2, starting transfers between devices, per_device(): lax.ppermute(part, 'exp', xor_pairs(exp_count, bits))  3.09 us
    ppermute x1, waiting for transfers between devices, spread(): lax.ppermute(v, 'ctx', pairs)  2.34 us
    pallas_call x1, Pallas kernels, w_down_quarter(): pl.pallas_call(quarter_kernel, out_shape=jax.ShapeDtypeStruct((units, wid...  1.6 us
  transfers between devices with their start and end apart: 12, of which 7 were waited for; matrix products, arithmetic and copies ran while one was open for 0% of the time, Pallas kernels for 41%

profile of v3, /device:TPU:14, one launch (start us, length us, event | category | flops | bytes accessed | tf_op | source)
XLA Modules:
  0.0 59.4 jit_solution(3359476245073833429)
XLA Ops:
  0.0 0.0 collective-permute-start.3
  0.0 0.5 collective-permute-start.4
  0.5 0.5 collective-permute-start.1
  1.0 1.5 %collective-permute-start.2 = (bf16[256,512]{1,0:T(8,128)(2,1)}, bf16[256,512]{1,0:T(8,128)(2,1)S(1)}, u32[]{:S(2)}, u32[]{:S(2)}) collective-permute-start(bf16[256,512]{1,0:T(8,128)(2,1)} %bitcast.20), channel_id=1, source_target_pairs={{0,8},{4,12},{8,0},{12,4},{1,9},{5,13},{9,1},{13,5},{2,10},{6,14},... | collective-permute-start | bytes 786440 | tf_op jit(solution)/shard_map/ppermute | solution.py:528
  2.5 0.1 stack.27.place_ref
  2.6 1.6 %shard_map.100 = bf16[304,896]{1,0:T(8,128)(2,1)S(1)} custom-call(s32[5]{0:T(128)S(1)} %stack.27.place_ref, bf16[304,3584]{1,0:T(8,128)(2,1)} %rest_14_.1), custom_call_target="tpu_custom_call" | custom-call | flops 304 | bytes 1089536 | tf_op jit(solution)/shard_map/pallas_call | solution.py:374
  4.2 0.5 collective-permute-start
  4.7 0.0 collective-permute-done.3.k_ref
  4.8 0.0 collective-permute-done.4.v_ref
  4.8 7.4 %shard_map.101 = (f32[4,896,128]{2,1,0:T(8,128)S(1)}, f32[4,896,128]{2,1,0:T(8,128)S(1)}, f32[4,896,128]{2,1,0:T(8,128)S(1)}, bf16[128,3584]{1,0:T(8,128)(2,1)S(...) custom-call(s32[1,8]{1,0:T(1,128)} %labels_ref.9, ...), custom_call_target="tpu_custom_call" | custom-call | flops 18790481920 | bytes 1835008 | tf_op jit(solution)/shard_map/pallas_call | solution.py:394
  12.2 0.0 collective-permute-done.1.rest_8_
  12.2 2.3 %collective-permute-done.2.rest_10_ = bf16[256,512]{1,0:T(8,128)(2,1)S(1)} collective-permute-done((bf16[256,512]{1,0:T(8,128)(2,1)}, bf16[256,512]{1,0:T(8,128)(2,1)S(1)}, u32[]{:S(2)}, u32[]{:S(2)}) %collective-permute-start.2) | collective-permute-done | bytes 262176 | tf_op jit(solution)/shard_map/ppermute | solution.py:528
  14.6 0.0 collective-permute-start.5
  14.6 0.5 collective-permute-start.6
  15.1 1.0 %collective-permute-done.5.rest_9_ = bf16[256,512]{1,0:T(8,128)(2,1)S(1)} collective-permute-done((bf16[256,512]{1,0:T(8,128)(2,1)S(1)}, bf16[256,512]{1,0:T(8,128)(2,1)S(1)}, u32[]{:S(2)}, u32[]{:S(2)}) %collective-permute-start.5) | collective-permute-done | bytes 262176 | tf_op jit(solution)/shard_map/ppermute | solution.py:531
  16.1 0.4 collective-permute-done.6.rest_11_
  16.5 11.7 %shard_map.102 = (bf16[192,304]{1,0:T(8,128)(2,1)S(1)}, bf16[256,304]{1,0:T(8,128)(2,1)S(1)}, f32[256,3584]{1,0:T(8,128)S(1)}, bf16[304,3584]{1,0:T(8,128)(2,1)S(1)}, bf16[64,1792]{1,0:T(8,128)(2,1)S(1)}) custom-call(s32[1,8]{1,0:T(1,128)} %labels_ref.9, s32[1,8,8]{2,1,0:T(8,128)} %mask_ref.3, s32[5]{0:T(128)S(1)} %stack.27.place_ref, ...), custom_call_target="tpu_custom_call" | custom-call | flops 917504 | bytes 3584 | tf_op jit(solution)/shard_map/pallas_call | solution.py:427
  28.2 0.0 collective-permute-done.here_ref
  28.2 0.5 collective-permute-start.7
  28.7 0.0 collective-permute-start.9
  28.7 1.1 %shard_map.103.base_ref = f32[128,1792]{1,0:T(8,128)S(1)} custom-call(s32[1,8]{1,0:T(1,128)} %labels_ref.9, s32[5]{0:T(128)S(1)} %stack.27.place_ref, bf16[256,304]{1,0:T(8,128)(2,1)S(1)} %get-tuple-element.43.hid_ref, f32[256,3584]{1,0:T(8,128)S(1)} %get-tuple-element.44.mid_ref, bf16[304,3584]{1,0:T(8,128)(2,1)S(1)} %get-tuple-element.45.wd_ref), custom_call_target="tpu_custom_call" | custom-call | flops 11156848640 | bytes 1089536 | tf_op jit(solution)/shard_map/pallas_call | solution.py:457
  29.8 4.4 %collective-permute-done.7.in_ref = bf16[192,304]{1,0:T(8,128)(2,1)S(1)} collective-permute-done((bf16[192,304]{1,0:T(8,128)(2,1)S(1)}, bf16[192,304]{1,0:T(8,128)(2,1)S(1)}, u32[]{:S(2)}, u32[]{:S(2)}) %collective-permute-start.7) | collective-permute-done | bytes 116768 | tf_op jit(solution)/shard_map/ppermute | solution.py:560
  34.2 0.5 collective-permute-start.8
  34.6 0.0 collective-permute-done.9.there_ref
  34.6 1.1 %shard_map.104 = (bf16[64,1792]{1,0:T(8,128)(2,1)S(1)}, bf16[64,1792]{1,0:T(8,128)(2,1)S(1)}, f32[8,128]{1,0:T(8,128)S(1)}) custom-call(s32[1,8]{1,0:T(1,128)} %labels_ref.9, s32[5]{0:T(128)S(1)} %stack.27.place_ref, bf16[192,304]{1,0:T(8,128)(2,1)S(1)} %collective-permute-done.7.in_ref, f32[128,1792]{1,0:T(8,128)S(1)} %shard_map.103.base_ref, ...), custom_call_target="tpu_custom_call" | custom-call | flops 128 | bytes 128 | tf_op jit(solution)/shard_map/pallas_call | solution.py:470
  35.7 0.1 collective-permute-start.10
  35.8 3.0 %collective-permute-start.11 = (bf16[64,1792]{1,0:T(8,128)(2,1)S(1)}, bf16[64,1792]{1,0:T(8,128)(2,1)S(1)}, u32[]{:S(2)}, u32[]{:S(2)}) collective-permute-start(bf16[64,1792]{1,0:T(8,128)(2,1)S(1)} %get-tuple-element.52), channel_id=1, source_target_pairs={{0,3},{1,2},{2,1},{3,0},{4,7},{5,6},{6,5},{7,4},{8,11},{9,10},{10,... | collective-permute-start | bytes 688136 | tf_op jit(solution)/shard_map/ppermute | solution.py:565
  38.8 3.9 %collective-permute-done.8.sum_ref = bf16[64,1792]{1,0:T(8,128)(2,1)S(1)} collective-permute-done((bf16[64,1792]{1,0:T(8,128)(2,1)S(1)}, bf16[64,1792]{1,0:T(8,128)(2,1)S(1)}, u32[]{:S(2)}, u32[]{:S(2)}) %collective-permute-start.8) | collective-permute-done | bytes 229408 | tf_op jit(solution)/shard_map/ppermute | solution.py:567
  42.7 1.5 %shard_map.105.staying_ref = f32[64,3584]{1,0:T(8,128)S(1)} custom-call(s32[1,8]{1,0:T(1,128)} %labels_ref.9, s32[5]{0:T(128)S(1)} %stack.27.place_ref, bf16[192,304]{1,0:T(8,128)(2,1)S(1)} %collective-permute-done.7.in_ref, bf16[256,304]{1,0:T(8,128)(2,1)S(1)} %get-tuple-element.43.hid_ref, f32[256,3584]{1,0:T(8,128)S(1)} %get-tuple-element.44.mid_ref, ...), custom_call_target="tpu_custom_call" | custom-call | flops 11156848640 | bytes 1089536 | tf_op jit(solution)/shard_map/pallas_call | solution.py:482
  44.2 7.5 %collective-permute-done.10.same_ref = bf16[64,1792]{1,0:T(8,128)(2,1)S(1)} collective-permute-done((bf16[64,1792]{1,0:T(8,128)(2,1)S(1)}, bf16[64,1792]{1,0:T(8,128)(2,1)S(1)}, u32[]{:S(2)}, u32[]{:S(2)}) %collective-permute-start.10) | collective-permute-done | bytes 229408 | tf_op jit(solution)/shard_map/ppermute | solution.py:565
  51.7 6.3 %collective-permute-done.11.other_ref = bf16[64,1792]{1,0:T(8,128)(2,1)S(1)} collective-permute-done((bf16[64,1792]{1,0:T(8,128)(2,1)S(1)}, bf16[64,1792]{1,0:T(8,128)(2,1)S(1)}, u32[]{:S(2)}, u32[]{:S(2)}) %collective-permute-start.11) | collective-permute-done | bytes 229408 | tf_op jit(solution)/shard_map/ppermute | solution.py:565
  58.0 1.4 %shard_map.106 = bf16[64,3584]{1,0:T(8,128)(2,1)} custom-call(s32[5]{0:T(128)S(1)} %stack.27.place_ref, f32[64,3584]{1,0:T(8,128)S(1)} %shard_map.105.staying_ref, bf16[64,1792]{1,0:T(8,128)(2,1)S(1)} %collective-permute-done.10.same_ref, bf16[64,1792]{1,0:T(8,128)(2,1)S(1)} %collective-permute-done.11.other_ref), custom_call_target="tpu_custom_call" | custom-call | flops 229376 | bytes 229376 | tf_op jit(solution)/shard_map/pallas_call | solution.py:493
Async XLA Ops:
  0.0 4.8 %collective-permute-start.3 = (bf16[256,512]{1,0:T(8,128)(2,1)}, bf16[256,512]{1,0:T(8,128)(2,1)S(1)}, u32[]{:S(2)}, u32[]{:S(2)}) collective-permute-start(bf16[256,512]{1,0:T(8,128)(2,1)} %bitcast.16), channel_id=1, source_target_pairs={{0,4},{4,0},{8,12},{12,8},{1,5},{5,1},{9,13},{13,9},{2,6},{6,2},{1... | collective-permute-start | bytes 786440 | tf_op jit(solution)/shard_map/ppermute | solution.py:531
  0.0 4.8 %collective-permute-start.4 = (bf16[256,512]{1,0:T(8,128)(2,1)}, bf16[256,512]{1,0:T(8,128)(2,1)S(1)}, u32[]{:S(2)}, u32[]{:S(2)}) collective-permute-start(bf16[256,512]{1,0:T(8,128)(2,1)} %bitcast.19), channel_id=1, source_target_pairs={{0,4},{4,0},{8,12},{12,8},{1,5},{5,1},{9,13},{13,9},{2,6},{6,2},{1... | collective-permute-start | bytes 786440 | tf_op jit(solution)/shard_map/ppermute | solution.py:531
  0.5 11.7 %collective-permute-start.1 = (bf16[256,512]{1,0:T(8,128)(2,1)}, bf16[256,512]{1,0:T(8,128)(2,1)S(1)}, u32[]{:S(2)}, u32[]{:S(2)}) collective-permute-start(bf16[256,512]{1,0:T(8,128)(2,1)} %bitcast.17), channel_id=1, source_target_pairs={{0,8},{4,12},{8,0},{12,4},{1,9},{5,13},{9,1},{13,5},{2,10},{6,14},... | collective-permute-start | bytes 786440 | tf_op jit(solution)/shard_map/ppermute | solution.py:528
  1.0 13.5 %collective-permute-start.2 = (bf16[256,512]{1,0:T(8,128)(2,1)}, bf16[256,512]{1,0:T(8,128)(2,1)S(1)}, u32[]{:S(2)}, u32[]{:S(2)}) collective-permute-start(bf16[256,512]{1,0:T(8,128)(2,1)} %bitcast.20), channel_id=1, source_target_pairs={{0,8},{4,12},{8,0},{12,4},{1,9},{5,13},{9,1},{13,5},{2,10},{6,14},... | collective-permute-start | bytes 786440 | tf_op jit(solution)/shard_map/ppermute | solution.py:528
  4.2 24.0 %collective-permute-start = (bf16[304,896]{1,0:T(8,128)(2,1)S(1)}, bf16[304,896]{1,0:T(8,128)(2,1)S(1)}, u32[]{:S(2)}, u32[]{:S(2)}) collective-permute-start(bf16[304,896]{1,0:T(8,128)(2,1)S(1)} %shard_map.100), channel_id=1, source_target_pairs={{0,1},{1,0},{2,3},{3,2},{4,5},{5,4},{6,7},{7,6},{8,9},{9,8},{10,11... | collective-permute-start | bytes 1634312 | tf_op jit(solution)/shard_map/ppermute | solution.py:540
  14.6 1.5 %collective-permute-start.5 = (bf16[256,512]{1,0:T(8,128)(2,1)S(1)}, bf16[256,512]{1,0:T(8,128)(2,1)S(1)}, u32[]{:S(2)}, u32[]{:S(2)}) collective-permute-start(bf16[256,512]{1,0:T(8,128)(2,1)S(1)} %collective-permute-done.1.rest_8_), channel_id=1, source_target_pairs={{0,4},{4,0},{8,12},{12,8},{1,5},{5,1},{9,13},{13,9},{2,6},{6,2},{1... | collective-permute-start | bytes 786440 | tf_op jit(solution)/shard_map/ppermute | solution.py:531
  14.6 1.9 %collective-permute-start.6 = (bf16[256,512]{1,0:T(8,128)(2,1)S(1)}, bf16[256,512]{1,0:T(8,128)(2,1)S(1)}, u32[]{:S(2)}, u32[]{:S(2)}) collective-permute-start(bf16[256,512]{1,0:T(8,128)(2,1)S(1)} %collective-permute-done.2.rest_10_), channel_id=1, source_target_pairs={{0,4},{4,0},{8,12},{12,8},{1,5},{5,1},{9,13},{13,9},{2,6},{6,2},{1... | collective-permute-start | bytes 786440 | tf_op jit(solution)/shard_map/ppermute | solution.py:531
  28.2 6.0 %collective-permute-start.7 = (bf16[192,304]{1,0:T(8,128)(2,1)S(1)}, bf16[192,304]{1,0:T(8,128)(2,1)S(1)}, u32[]{:S(2)}, u32[]{:S(2)}) collective-permute-start(bf16[192,304]{1,0:T(8,128)(2,1)S(1)} %get-tuple-element.41), channel_id=1, source_target_pairs={{0,1},{1,0},{2,3},{3,2},{4,5},{5,4},{6,7},{7,6},{8,9},{9,8},{10,11... | collective-permute-start | bytes 350216 | tf_op jit(solution)/shard_map/ppermute | solution.py:560
  28.7 5.9 %collective-permute-start.9 = (bf16[304,896]{1,0:T(8,128)(2,1)S(1)}, bf16[304,896]{1,0:T(8,128)(2,1)S(1)}, u32[]{:S(2)}, u32[]{:S(2)}) collective-permute-start(bf16[304,896]{1,0:T(8,128)(2,1)S(1)} %collective-permute-done.here_ref), channel_id=1, source_target_pairs={{0,4},{4,0},{8,12},{12,8},{1,5},{5,1},{9,13},{13,9},{2,6},{6,2},{1... | collective-permute-start | bytes 1634312 | tf_op jit(solution)/shard_map/ppermute | solution.py:531
  34.2 8.5 %collective-permute-start.8 = (bf16[64,1792]{1,0:T(8,128)(2,1)S(1)}, bf16[64,1792]{1,0:T(8,128)(2,1)S(1)}, u32[]{:S(2)}, u32[]{:S(2)}) collective-permute-start(bf16[64,1792]{1,0:T(8,128)(2,1)S(1)} %get-tuple-element.47), channel_id=1, source_target_pairs={{0,1},{1,0},{2,3},{3,2},{4,5},{5,4},{6,7},{7,6},{8,9},{9,8},{10,11... | collective-permute-start | bytes 688136 | tf_op jit(solution)/shard_map/ppermute | solution.py:567
  35.7 16.0 %collective-permute-start.10 = (bf16[64,1792]{1,0:T(8,128)(2,1)S(1)}, bf16[64,1792]{1,0:T(8,128)(2,1)S(1)}, u32[]{:S(2)}, u32[]{:S(2)}) collective-permute-start(bf16[64,1792]{1,0:T(8,128)(2,1)S(1)} %get-tuple-element.51), channel_id=1, source_target_pairs={{0,2},{1,3},{2,0},{3,1},{4,6},{5,7},{6,4},{7,5},{8,10},{9,11},{10,... | collective-permute-start | bytes 688136 | tf_op jit(solution)/shard_map/ppermute | solution.py:565
  35.8 22.2 %collective-permute-start.11 = (bf16[64,1792]{1,0:T(8,128)(2,1)S(1)}, bf16[64,1792]{1,0:T(8,128)(2,1)S(1)}, u32[]{:S(2)}, u32[]{:S(2)}) collective-permute-start(bf16[64,1792]{1,0:T(8,128)(2,1)S(1)} %get-tuple-element.52), channel_id=1, source_target_pairs={{0,3},{1,2},{2,1},{3,0},{4,7},{5,6},{6,5},{7,4},{8,11},{9,10},{10,... | collective-permute-start | bytes 688136 | tf_op jit(solution)/shard_map/ppermute | solution.py:565

commit v4 on v3

--- a/solution.py
+++ b/solution.py
@@ -559,7 +559,7 @@
     there = swap(here)
     arrived = lax.ppermute(send, "exp", z_pairs)
     base = down_own(labels, place, hid, mid, own_wd)
-    arrived, sent, base = lax.optimization_barrier((arrived, sent, base))
+    sent, there = lax.optimization_barrier((sent, there))
     same, other, token = down_leave(labels, place, arrived, base, here, there)
     same, other = (
         lax.ppermute(part, "exp", xor_pairs(exp_count, bits)) for part, bits in ((same, 2), (other, 3))

time: 58.3 us -> 58.9 us (1.010); the launches traced: 59.4 us -> 59 us
  starting transfers between devices: 7.62 us -> 6.55 us
  waiting for transfers between devices: 25.8 us -> 26.4 us
    ppermute x2, waiting for transfers between devices: 13.8 us -> 16.2 us  [per_device(): lax.ppermute(part, 'exp', xor_pairs(exp_count, bits))]
    ppermute x1, waiting for transfers between devices: 3.88 us -> 1.84 us  [per_device(): summed = lax.ppermute(sent, 'exp', z_pairs)]
    ppermute x5, waiting for transfers between devices: 1.41 us -> 2.82 us  [swap(): return lax.ppermute(array, 'ctx', xor_pairs(ctx_count, 1))]
    ppermute x2, starting transfers between devices: 3.09 us -> 1.96 us  [per_device(): lax.ppermute(part, 'exp', xor_pairs(exp_count, bits))]
    ppermute x1, waiting for transfers between devices: 4.36 us -> 3.27 us  [per_device(): arrived = lax.ppermute(send, 'exp', z_pairs)]
  transfers between devices with their start and end apart: 12 -> 12, of which waited for: 7 -> 8; matrix products, arithmetic and copies ran while one was open for 0% -> 0% of each run, Pallas kernels for 41% -> 41%
where the time goes in v4:
time: 58.9 us; the launch traced here: 59 us
  waiting for transfers between devices  26.4 us (45%)
  Pallas kernels  25.8 us (44%)
  starting transfers between devices  6.55 us (11%)
    ppermute x2, waiting for transfers between devices, per_device(): lax.ppermute(part, 'exp', xor_pairs(exp_count, bits))  16.2 us
    pallas_call x1, Pallas kernels, far_attention(): pl.pallas_call(functools.partial(far_kernel, split, pieces), out_shape=ou...  11.7 us
    pallas_call x1, Pallas kernels, near_attention(): pl.pallas_call(functools.partial(near_kernel, split), out_shape=outs, in_...  7.44 us
    ppermute x1, waiting for transfers between devices, per_device(): arrived = lax.ppermute(send, 'exp', z_pairs)  3.27 us
    ppermute x5, waiting for transfers between devices, swap(): return lax.ppermute(array, 'ctx', xor_pairs(ctx_count, 1))  2.82 us
    ppermute x1, waiting for transfers between devices, spread(): lax.ppermute(v, 'ctx', pairs)  2.34 us
    ppermute x2, starting transfers between devices, per_device(): lax.ppermute(part, 'exp', xor_pairs(exp_count, bits))  1.96 us
    ppermute x1, waiting for transfers between devices, per_device(): summed = lax.ppermute(sent, 'exp', z_pairs)  1.84 us
  transfers between devices with their start and end apart: 12, of which 8 were waited for; matrix products, arithmetic and copies ran while one was open for 0% of the time, Pallas kernels for 41%

profile of v4, /device:TPU:14, one launch (start us, length us, event | category | flops | bytes accessed | tf_op | source)
XLA Modules:
  0.0 59.0 jit_solution(17901043123051247423)
XLA Ops:
  0.0 0.0 collective-permute-start.3
  0.0 0.5 collective-permute-start.4
  0.5 0.5 collective-permute-start.1
  1.0 1.5 %collective-permute-start.2 = (bf16[256,512]{1,0:T(8,128)(2,1)}, bf16[256,512]{1,0:T(8,128)(2,1)S(1)}, u32[]{:S(2)}, u32[]{:S(2)}) collective-permute-start(bf16[256,512]{1,0:T(8,128)(2,1)} %bitcast.20), channel_id=1, source_target_pairs={{0,8},{4,12},{8,0},{12,4},{1,9},{5,13},{9,1},{13,5},{2,10},{6,14},... | collective-permute-start | bytes 786440 | tf_op jit(solution)/shard_map/ppermute | solution.py:528
  2.5 0.1 stack.27.place_ref
  2.6 1.6 %shard_map.100 = bf16[304,896]{1,0:T(8,128)(2,1)S(1)} custom-call(s32[5]{0:T(128)S(1)} %stack.27.place_ref, bf16[304,3584]{1,0:T(8,128)(2,1)} %rest_14_.1), custom_call_target="tpu_custom_call" | custom-call | flops 304 | bytes 1089536 | tf_op jit(solution)/shard_map/pallas_call | solution.py:374
  4.2 0.5 collective-permute-start
  4.7 0.0 collective-permute-done.3.k_ref
  4.8 0.0 collective-permute-done.4.v_ref
  4.8 7.4 %shard_map.101 = (f32[4,896,128]{2,1,0:T(8,128)S(1)}, f32[4,896,128]{2,1,0:T(8,128)S(1)}, f32[4,896,128]{2,1,0:T(8,128)S(1)}, bf16[128,3584]{1,0:T(8,128)(2,1)S(...) custom-call(s32[1,8]{1,0:T(1,128)} %labels_ref.9, ...), custom_call_target="tpu_custom_call" | custom-call | flops 18790481920 | bytes 1835008 | tf_op jit(solution)/shard_map/pallas_call | solution.py:394
  12.2 0.0 collective-permute-done.1.rest_8_
  12.2 2.3 %collective-permute-done.2.rest_10_ = bf16[256,512]{1,0:T(8,128)(2,1)S(1)} collective-permute-done((bf16[256,512]{1,0:T(8,128)(2,1)}, bf16[256,512]{1,0:T(8,128)(2,1)S(1)}, u32[]{:S(2)}, u32[]{:S(2)}) %collective-permute-start.2) | collective-permute-done | bytes 262176 | tf_op jit(solution)/shard_map/ppermute | solution.py:528
  14.6 0.0 collective-permute-start.5
  14.6 0.5 collective-permute-start.6
  15.1 1.0 %collective-permute-done.5.rest_9_ = bf16[256,512]{1,0:T(8,128)(2,1)S(1)} collective-permute-done((bf16[256,512]{1,0:T(8,128)(2,1)S(1)}, bf16[256,512]{1,0:T(8,128)(2,1)S(1)}, u32[]{:S(2)}, u32[]{:S(2)}) %collective-permute-start.5) | collective-permute-done | bytes 262176 | tf_op jit(solution)/shard_map/ppermute | solution.py:531
  16.1 0.4 collective-permute-done.6.rest_11_
  16.5 11.7 %shard_map.102 = (bf16[192,304]{1,0:T(8,128)(2,1)S(1)}, bf16[256,304]{1,0:T(8,128)(2,1)S(1)}, f32[256,3584]{1,0:T(8,128)S(1)}, bf16[304,3584]{1,0:T(8,128)(2,1)S(1)}, bf16[64,1792]{1,0:T(8,128)(2,1)S(1)}) custom-call(s32[1,8]{1,0:T(1,128)} %labels_ref.9, s32[1,8,8]{2,1,0:T(8,128)} %mask_ref.3, s32[5]{0:T(128)S(1)} %stack.27.place_ref, ...), custom_call_target="tpu_custom_call" | custom-call | flops 917504 | bytes 3584 | tf_op jit(solution)/shard_map/pallas_call | solution.py:427
  28.2 0.0 collective-permute-done.here_ref
  28.2 0.1 collective-permute-start.8
  28.3 0.5 collective-permute-start.7
  28.8 1.4 %collective-permute-done.8.there_ref = bf16[304,896]{1,0:T(8,128)(2,1)S(1)} collective-permute-done((bf16[304,896]{1,0:T(8,128)(2,1)S(1)}, bf16[304,896]{1,0:T(8,128)(2,1)S(1)}, u32[]{:S(2)}, u32[]{:S(2)}) %collective-permute-start.8) | collective-permute-done | bytes 544800 | tf_op jit(solution)/shard_map/ppermute | solution.py:531
  30.2 0.4 collective-permute-start.9
  30.7 1.1 %shard_map.103.base_ref = f32[128,1792]{1,0:T(8,128)S(1)} custom-call(s32[1,8]{1,0:T(1,128)} %labels_ref.9, s32[5]{0:T(128)S(1)} %stack.27.place_ref, bf16[256,304]{1,0:T(8,128)(2,1)S(1)} %get-tuple-element.41.hid_ref, f32[256,3584]{1,0:T(8,128)S(1)} %get-tuple-element.42.mid_ref, bf16[304,3584]{1,0:T(8,128)(2,1)S(1)} %get-tuple-element.43.wd_ref), custom_call_target="tpu_custom_call" | custom-call | flops 11156848640 | bytes 1089536 | tf_op jit(solution)/shard_map/pallas_call | solution.py:457
  31.7 3.3 %collective-permute-done.7.in_ref = bf16[192,304]{1,0:T(8,128)(2,1)S(1)} collective-permute-done((bf16[192,304]{1,0:T(8,128)(2,1)S(1)}, bf16[192,304]{1,0:T(8,128)(2,1)S(1)}, u32[]{:S(2)}, u32[]{:S(2)}) %collective-permute-start.7) | collective-permute-done | bytes 116768 | tf_op jit(solution)/shard_map/ppermute | solution.py:560
  35.0 1.1 %shard_map.104 = (bf16[64,1792]{1,0:T(8,128)(2,1)S(1)}, bf16[64,1792]{1,0:T(8,128)(2,1)S(1)}, f32[8,128]{1,0:T(8,128)S(1)}) custom-call(s32[1,8]{1,0:T(1,128)} %labels_ref.9, s32[5]{0:T(128)S(1)} %stack.27.place_ref, bf16[192,304]{1,0:T(8,128)(2,1)S(1)} %collective-permute-done.7.in_ref, f32[128,1792]{1,0:T(8,128)S(1)} %shard_map.103.base_ref, ...), custom_call_target="tpu_custom_call" | custom-call | flops 128 | bytes 128 | tf_op jit(solution)/shard_map/pallas_call | solution.py:470
  36.1 0.1 collective-permute-start.10
  36.2 1.9 %collective-permute-start.11 = (bf16[64,1792]{1,0:T(8,128)(2,1)S(1)}, bf16[64,1792]{1,0:T(8,128)(2,1)S(1)}, u32[]{:S(2)}, u32[]{:S(2)}) collective-permute-start(bf16[64,1792]{1,0:T(8,128)(2,1)S(1)} %get-tuple-element.50), channel_id=1, source_target_pairs={{0,3},{1,2},{2,1},{3,0},{4,7},{5,6},{6,5},{7,4},{8,11},{9,10},{10,... | collective-permute-start | bytes 688136 | tf_op jit(solution)/shard_map/ppermute | solution.py:565
  38.1 1.8 %collective-permute-done.9.sum_ref = bf16[64,1792]{1,0:T(8,128)(2,1)S(1)} collective-permute-done((bf16[64,1792]{1,0:T(8,128)(2,1)S(1)}, bf16[64,1792]{1,0:T(8,128)(2,1)S(1)}, u32[]{:S(2)}, u32[]{:S(2)}) %collective-permute-start.9) | collective-permute-done | bytes 229408 | tf_op jit(solution)/shard_map/ppermute | solution.py:567
  39.9 1.5 %shard_map.105.staying_ref = f32[64,3584]{1,0:T(8,128)S(1)} custom-call(s32[1,8]{1,0:T(1,128)} %labels_ref.9, s32[5]{0:T(128)S(1)} %stack.27.place_ref, bf16[192,304]{1,0:T(8,128)(2,1)S(1)} %collective-permute-done.7.in_ref, bf16[256,304]{1,0:T(8,128)(2,1)S(1)} %get-tuple-element.41.hid_ref, f32[256,3584]{1,0:T(8,128)S(1)} %get-tuple-element.42.mid_ref, ...), custom_call_target="tpu_custom_call" | custom-call | flops 11156848640 | bytes 1089536 | tf_op jit(solution)/shard_map/pallas_call | solution.py:482
  41.4 10.7 %collective-permute-done.10.same_ref = bf16[64,1792]{1,0:T(8,128)(2,1)S(1)} collective-permute-done((bf16[64,1792]{1,0:T(8,128)(2,1)S(1)}, bf16[64,1792]{1,0:T(8,128)(2,1)S(1)}, u32[]{:S(2)}, u32[]{:S(2)}) %collective-permute-start.10) | collective-permute-done | bytes 229408 | tf_op jit(solution)/shard_map/ppermute | solution.py:565
  52.1 5.5 %collective-permute-done.11.other_ref = bf16[64,1792]{1,0:T(8,128)(2,1)S(1)} collective-permute-done((bf16[64,1792]{1,0:T(8,128)(2,1)S(1)}, bf16[64,1792]{1,0:T(8,128)(2,1)S(1)}, u32[]{:S(2)}, u32[]{:S(2)}) %collective-permute-start.11) | collective-permute-done | bytes 229408 | tf_op jit(solution)/shard_map/ppermute | solution.py:565
  57.6 1.4 %shard_map.106 = bf16[64,3584]{1,0:T(8,128)(2,1)} custom-call(s32[5]{0:T(128)S(1)} %stack.27.place_ref, f32[64,3584]{1,0:T(8,128)S(1)} %shard_map.105.staying_ref, bf16[64,1792]{1,0:T(8,128)(2,1)S(1)} %collective-permute-done.10.same_ref, bf16[64,1792]{1,0:T(8,128)(2,1)S(1)} %collective-permute-done.11.other_ref), custom_call_target="tpu_custom_call" | custom-call | flops 229376 | bytes 229376 | tf_op jit(solution)/shard_map/pallas_call | solution.py:493
Async XLA Ops:
  0.0 4.8 %collective-permute-start.3 = (bf16[256,512]{1,0:T(8,128)(2,1)}, bf16[256,512]{1,0:T(8,128)(2,1)S(1)}, u32[]{:S(2)}, u32[]{:S(2)}) collective-permute-start(bf16[256,512]{1,0:T(8,128)(2,1)} %bitcast.16), channel_id=1, source_target_pairs={{0,4},{4,0},{8,12},{12,8},{1,5},{5,1},{9,13},{13,9},{2,6},{6,2},{1... | collective-permute-start | bytes 786440 | tf_op jit(solution)/shard_map/ppermute | solution.py:531
  0.0 4.8 %collective-permute-start.4 = (bf16[256,512]{1,0:T(8,128)(2,1)}, bf16[256,512]{1,0:T(8,128)(2,1)S(1)}, u32[]{:S(2)}, u32[]{:S(2)}) collective-permute-start(bf16[256,512]{1,0:T(8,128)(2,1)} %bitcast.19), channel_id=1, source_target_pairs={{0,4},{4,0},{8,12},{12,8},{1,5},{5,1},{9,13},{13,9},{2,6},{6,2},{1... | collective-permute-start | bytes 786440 | tf_op jit(solution)/shard_map/ppermute | solution.py:531
  0.5 11.7 %collective-permute-start.1 = (bf16[256,512]{1,0:T(8,128)(2,1)}, bf16[256,512]{1,0:T(8,128)(2,1)S(1)}, u32[]{:S(2)}, u32[]{:S(2)}) collective-permute-start(bf16[256,512]{1,0:T(8,128)(2,1)} %bitcast.17), channel_id=1, source_target_pairs={{0,8},{4,12},{8,0},{12,4},{1,9},{5,13},{9,1},{13,5},{2,10},{6,14},... | collective-permute-start | bytes 786440 | tf_op jit(solution)/shard_map/ppermute | solution.py:528
  1.0 13.5 %collective-permute-start.2 = (bf16[256,512]{1,0:T(8,128)(2,1)}, bf16[256,512]{1,0:T(8,128)(2,1)S(1)}, u32[]{:S(2)}, u32[]{:S(2)}) collective-permute-start(bf16[256,512]{1,0:T(8,128)(2,1)} %bitcast.20), channel_id=1, source_target_pairs={{0,8},{4,12},{8,0},{12,4},{1,9},{5,13},{9,1},{13,5},{2,10},{6,14},... | collective-permute-start | bytes 786440 | tf_op jit(solution)/shard_map/ppermute | solution.py:528
  4.2 24.0 %collective-permute-start = (bf16[304,896]{1,0:T(8,128)(2,1)S(1)}, bf16[304,896]{1,0:T(8,128)(2,1)S(1)}, u32[]{:S(2)}, u32[]{:S(2)}) collective-permute-start(bf16[304,896]{1,0:T(8,128)(2,1)S(1)} %shard_map.100), channel_id=1, source_target_pairs={{0,1},{1,0},{2,3},{3,2},{4,5},{5,4},{6,7},{7,6},{8,9},{9,8},{10,11... | collective-permute-start | bytes 1634312 | tf_op jit(solution)/shard_map/ppermute | solution.py:540
  14.6 1.5 %collective-permute-start.5 = (bf16[256,512]{1,0:T(8,128)(2,1)S(1)}, bf16[256,512]{1,0:T(8,128)(2,1)S(1)}, u32[]{:S(2)}, u32[]{:S(2)}) collective-permute-start(bf16[256,512]{1,0:T(8,128)(2,1)S(1)} %collective-permute-done.1.rest_8_), channel_id=1, source_target_pairs={{0,4},{4,0},{8,12},{12,8},{1,5},{5,1},{9,13},{13,9},{2,6},{6,2},{1... | collective-permute-start | bytes 786440 | tf_op jit(solution)/shard_map/ppermute | solution.py:531
  14.6 1.9 %collective-permute-start.6 = (bf16[256,512]{1,0:T(8,128)(2,1)S(1)}, bf16[256,512]{1,0:T(8,128)(2,1)S(1)}, u32[]{:S(2)}, u32[]{:S(2)}) collective-permute-start(bf16[256,512]{1,0:T(8,128)(2,1)S(1)} %collective-permute-done.2.rest_10_), channel_id=1, source_target_pairs={{0,4},{4,0},{8,12},{12,8},{1,5},{5,1},{9,13},{13,9},{2,6},{6,2},{1... | collective-permute-start | bytes 786440 | tf_op jit(solution)/shard_map/ppermute | solution.py:531
  28.2 2.0 %collective-permute-start.8 = (bf16[304,896]{1,0:T(8,128)(2,1)S(1)}, bf16[304,896]{1,0:T(8,128)(2,1)S(1)}, u32[]{:S(2)}, u32[]{:S(2)}) collective-permute-start(bf16[304,896]{1,0:T(8,128)(2,1)S(1)} %collective-permute-done.here_ref), channel_id=1, source_target_pairs={{0,4},{4,0},{8,12},{12,8},{1,5},{5,1},{9,13},{13,9},{2,6},{6,2},{1... | collective-permute-start | bytes 1634312 | tf_op jit(solution)/shard_map/ppermute | solution.py:531
  28.3 6.7 %collective-permute-start.7 = (bf16[192,304]{1,0:T(8,128)(2,1)S(1)}, bf16[192,304]{1,0:T(8,128)(2,1)S(1)}, u32[]{:S(2)}, u32[]{:S(2)}) collective-permute-start(bf16[192,304]{1,0:T(8,128)(2,1)S(1)} %get-tuple-element.40), channel_id=1, source_target_pairs={{0,1},{1,0},{2,3},{3,2},{4,5},{5,4},{6,7},{7,6},{8,9},{9,8},{10,11... | collective-permute-start | bytes 350216 | tf_op jit(solution)/shard_map/ppermute | solution.py:560
  30.2 9.7 %collective-permute-start.9 = (bf16[64,1792]{1,0:T(8,128)(2,1)S(1)}, bf16[64,1792]{1,0:T(8,128)(2,1)S(1)}, u32[]{:S(2)}, u32[]{:S(2)}) collective-permute-start(bf16[64,1792]{1,0:T(8,128)(2,1)S(1)} %get-tuple-element.46), channel_id=1, source_target_pairs={{0,1},{1,0},{2,3},{3,2},{4,5},{5,4},{6,7},{7,6},{8,9},{9,8},{10,11... | collective-permute-start | bytes 688136 | tf_op jit(solution)/shard_map/ppermute | solution.py:567
  36.1 16.0 %collective-permute-start.10 = (bf16[64,1792]{1,0:T(8,128)(2,1)S(1)}, bf16[64,1792]{1,0:T(8,128)(2,1)S(1)}, u32[]{:S(2)}, u32[]{:S(2)}) collective-permute-start(bf16[64,1792]{1,0:T(8,128)(2,1)S(1)} %get-tuple-element.49), channel_id=1, source_target_pairs={{0,2},{1,3},{2,0},{3,1},{4,6},{5,7},{6,4},{7,5},{8,10},{9,11},{10,... | collective-permute-start | bytes 688136 | tf_op jit(solution)/shard_map/ppermute | solution.py:565
  36.2 21.4 %collective-permute-start.11 = (bf16[64,1792]{1,0:T(8,128)(2,1)S(1)}, bf16[64,1792]{1,0:T(8,128)(2,1)S(1)}, u32[]{:S(2)}, u32[]{:S(2)}) collective-permute-start(bf16[64,1792]{1,0:T(8,128)(2,1)S(1)} %get-tuple-element.50), channel_id=1, source_target_pairs={{0,3},{1,2},{2,1},{3,0},{4,7},{5,6},{6,5},{7,4},{8,11},{9,10},{10,... | collective-permute-start | bytes 688136 | tf_op jit(solution)/shard_map/ppermute | solution.py:565
